TPU v7x, 32 devices: a whole 2x2x4 slice. The times are simulated.
32 devices in a mesh: seq: 32 (over z, y, x, core).
Axes of the slice: x: 2, y: 2, z: 4, core: 2. Of those that a mesh axis runs over, the one named last changes fastest.
Arguments:
- inputs: bfloat16 [32768, 768], P('seq'), may hold values from -6 to 6
- weight_one: bfloat16 [768, 3, 768], P('seq'), may hold values from -0.125 to 0.125
- weight_two: bfloat16 [768, 3, 768], P('seq'), may hold values from -0.125 to 0.125
- cotangent: bfloat16 [32768, 768], P('seq'), may hold values from -6 to 6
Outputs:
- outputs: bfloat16 [32768, 768], P('seq')
- input_grad: bfloat16 [32768, 768], P('seq')
- grad_one: float32 [768, 3, 768], P('seq')
- grad_two: float32 [768, 3, 768], P('seq')
All inputs are finite; a program needn't handle non-finite values.
Results may differ from a plain program's by a relative error of at most 0.0056.
Values may be sent and summed in bfloat16 or wider, within the bound.
No kernel may reach another device: no remote copies, remote signals or barrier semaphores. Data moves between devices by JAX's collectives and lax.ppermute only.
A program may use at most 128 MiB of HBM per device.

v0:
```python
import math

import jax
import jax.numpy as jnp
from jax import lax
from jax.experimental import pallas as pl
from jax.experimental.pallas import tpu as pltpu
from jax.sharding import PartitionSpec as P

DILATION_A = 32
DILATION_B = 64
HALO = DILATION_A + DILATION_B


def routes_of(count):
    bits = [1 << k for k in range(count.bit_length() - 2, 0, -1)]
    if len(bits) < 4:
        return [(bits, bits), (bits, bits)]
    far, (depth, row, column) = bits[:-3], bits[-3:]
    first = (far + [depth, column, row], far + [depth, row, column])
    second = (far + [column, depth, row], far + [row, depth, column])
    return [first, second]


def step_pairs(count, route, step):
    return [(i, i ^ route[i & 1][step]) for i in range(count)]


def core_pairs(count):
    return [(i, i ^ 1) for i in range(count)]


def relative_channels(count, route, block):
    position = jnp.arange(count * block)
    me = lax.axis_index("seq")
    index, offset = position // block, position % block
    half = count // 2
    other = index // half
    inner = index % half
    core = (me & 1) ^ other
    source = me ^ other
    for step in range(len(route[0])):
        bit = jnp.where(core == 0, route[0][step], route[1][step])
        source = source ^ jnp.where((inner >> step) & 1 == 1, bit, 0)
    return source * block + offset


def one_hot(count, route, block):
    channels = relative_channels(count, route, block)
    rows = lax.broadcasted_iota(jnp.int32, (count * block, count * block), 0)
    return (rows == channels[None, :]).astype(jnp.bfloat16)


def after(value, *others):
    return lax.optimization_barrier((value,) + others)[0]


class Gather:
    def __init__(self, shard, route):
        self.held = jnp.transpose(shard, (1, 0, 2))
        self.route = route
        self.steps = len(route[0])
        self.step = 0
        self.pieces = []

    def send(self):
        count = lax.axis_size("seq")
        if self.step < self.steps:
            self.arrived = lax.ppermute(self.held, "seq", step_pairs(count, self.route, self.step))
        if self.step >= self.steps - 1:
            self.pieces.append((self.held, lax.ppermute(self.held, "seq", core_pairs(count))))
        self.step += 1

    def join(self, *others):
        arrived = after(self.arrived, *others)
        if self.step < self.steps:
            arrived = join_rows(self.held, arrived)
        self.held = lax.optimization_barrier(arrived)
        return self.held

    def full(self):
        own, other = zip(*self.pieces)
        return own + other


class Scatter:
    def __init__(self, sends, route):
        self.route = route
        self.left = list(reversed(range(len(route[0]))))
        pairs = core_pairs(lax.axis_size("seq"))
        self.arrived = [lax.ppermute(send, "seq", pairs) for send in sends]

    def keep(self, keep):
        self.kept = keep

    def add(self, *others):
        arrived = self.arrived
        if isinstance(arrived, list):
            arrived = jnp.stack(lax.optimization_barrier(tuple(arrived) + others)[:3])
        else:
            arrived = after(arrived, *others)
        half = self.kept.shape[1] // 2
        send = (self.kept[:, half:] + arrived[:, half:].astype(jnp.float32)).astype(jnp.bfloat16)
        keep = self.kept[:, :half] + arrived[:, :half].astype(jnp.float32)
        send, self.kept = lax.optimization_barrier((send, keep))
        pairs = step_pairs(lax.axis_size("seq"), self.route, self.left.pop(0))
        self.arrived = lax.ppermute(send, "seq", pairs)
        return send

    def finish(self, grad_scale):
        return jnp.transpose((self.kept + self.arrived.astype(jnp.float32)) * grad_scale, (1, 0, 2))


def permute_channels(values, matrix, dim):
    return lax.dot_general(
        values, matrix, (((1,), (dim,)), ((), ())), preferred_element_type=jnp.float32
    ).astype(jnp.bfloat16)


CHUNK = 16
BLOCKS = 4
FREE = pl.CostEstimate(flops=0, bytes_accessed=0, transcendentals=0)


def on_chip(*arrays):
    return [pltpu.with_memory_space_constraint(array, pltpu.VMEM) for array in arrays]


def call(kernel, name, arrays, outs, scratch=(), edges=None, room=8):
    scalars = [] if edges is None else [edges]
    return pl.pallas_call(
        kernel,
        in_specs=[pl.BlockSpec(memory_space=pltpu.SMEM)] * len(scalars)
        + [pl.BlockSpec(memory_space=pltpu.VMEM)] * len(arrays),
        out_specs=[pl.BlockSpec(memory_space=pltpu.VMEM)] * len(outs),
        out_shape=[pltpu.VMEM(shape, dtype) for shape, dtype in outs],
        scratch_shapes=list(scratch),
        compiler_params=pltpu.CompilerParams(vmem_limit_bytes=room * 2**20),
        cost_estimate=FREE,
        name=name,
    )(*scalars, *on_chip(*arrays))


def over_blocks(length, body, unrolled):
    rows = length // BLOCKS

    def step(index, carry):
        body(index * rows, rows)
        return carry

    if unrolled:
        for index in range(BLOCKS):
            body(index * rows, rows)
    else:
        lax.fori_loop(0, BLOCKS, step, 0)


def span(first, rows):
    return pl.ds(first if isinstance(first, int) else pl.multiple_of(first, CHUNK), rows)


def inverse_rms(values):
    return lax.rsqrt(jnp.mean(values * values, axis=-1, keepdims=True) + 1e-06)


def cumulative_of(normed):
    return 0.5 * (1.0 + lax.erf(normed * 0.7071067811865476))


def activate(first, rel_ref, active_ref):
    for start in range(0, rel_ref.shape[0], CHUNK):
        values = rel_ref[start : start + CHUNK].astype(jnp.float32)
        normed = values * inverse_rms(values)
        active_ref[span(first + start, CHUNK)] = (normed * cumulative_of(normed)).astype(jnp.bfloat16)


def inside(edge_ref, first, rows):
    row = first + lax.broadcasted_iota(jnp.int32, (rows, 1), 0)
    return (row >= edge_ref[0]) & (row < edge_ref[1])


def join_kernel(first_ref, second_ref, out_ref):
    rows = first_ref.shape[1]
    out_ref[:, :rows] = first_ref[...]
    out_ref[:, rows:] = second_ref[...]


def join_rows(first, second):
    taps, rows, channels = first.shape
    if rows % 16:
        return jnp.concatenate([first, second], axis=1)
    shape = (taps, 2 * rows, channels)
    return call(join_kernel, "join_rows", [first, second], [(shape, first.dtype)], room=4)[0]


def active_kernel(
    odd_ref, layer_in_ref, grad_ref, inner_ref, outer_ref, turn_ref, next_turn_ref,
    wide_in_ref, wide_grad_ref, active_ref, grad_rel_ref, rel_ref, *, offset
):
    length = layer_in_ref.shape[0]
    halo = inner_ref.shape[0] // 2
    odd = odd_ref[0] == 1
    for index, (wide_ref, own_ref) in enumerate(((wide_in_ref, layer_in_ref), (wide_grad_ref, grad_ref))):
        rows = slice(index * halo, (index + 1) * halo)
        wide_ref[:halo] = jnp.where(odd, inner_ref[rows], outer_ref[rows])
        wide_ref[halo : halo + length] = own_ref[...]
        wide_ref[halo + length :] = jnp.where(odd, outer_ref[rows], inner_ref[rows])

    def own_block(first, rows):
        rel_ref[...] = jnp.dot(
            wide_in_ref[span(first, rows)], turn_ref[...], preferred_element_type=jnp.float32
        ).astype(jnp.bfloat16)
        activate(first, rel_ref, active_ref)

    def grad_block(first, rows):
        grad_rel_ref[span(first, rows)] = jnp.dot(
            wide_grad_ref[span(offset + first, rows)],
            next_turn_ref[...],
            preferred_element_type=jnp.float32,
        ).astype(jnp.bfloat16)

    over_blocks(wide_in_ref.shape[0], own_block, False)
    over_blocks(grad_rel_ref.shape[0], grad_block, False)


def first_active(odd, layer_in, grad, inner, outer, turn, next_turn, offset, back_rows):
    length, channels = layer_in.shape
    rows = length + inner.shape[0]
    wide = ((rows, channels), jnp.bfloat16)
    return call(
        lambda *refs: active_kernel(*refs, offset=offset),
        "first_active",
        [layer_in, grad, inner, outer, turn, next_turn],
        [wide, wide, wide, ((back_rows, channels), jnp.bfloat16)],
        [pltpu.VMEM((rows // BLOCKS, channels), jnp.bfloat16)],
        odd,
        room=6,
    )


def layer_kernel(edge_ref, *refs, spacing, offset, follow):
    pieces, (active_ref, layer_in_ref, *refs) = refs[:4], refs[4:]
    if follow:
        turn_ref, out_ref, rel_ref, next_ref, weight = refs
    else:
        out_ref, weight = refs
    length, channels = out_ref.shape
    size = channels // 4
    for tap in range(3):
        for index, piece in enumerate(pieces):
            first = tap * channels + index * size
            weight[first : first + size] = piece[tap]

    def block(first, rows):
        windows = [active_ref[span(first + tap * spacing, rows)] for tap in range(3)]
        mixed = jnp.dot(
            jnp.concatenate(windows, axis=1), weight[...], preferred_element_type=jnp.float32
        )
        out = layer_in_ref[span(offset + first, rows)].astype(jnp.float32) + mixed
        if follow:
            out = jnp.where(inside(edge_ref, first, rows), out, 0.0)
        out = out.astype(jnp.bfloat16)
        out_ref[span(first, rows)] = out
        if follow:
            rel_ref[span(first, rows)] = jnp.dot(
                out, turn_ref[...], preferred_element_type=jnp.float32
            ).astype(jnp.bfloat16)
            activate(first, rel_ref.at[span(first, rows)], next_ref)

    over_blocks(length, block, follow)


def layer(edges, pieces, active, layer_in, offset, length, spacing, turn=None):
    channels = active.shape[1]
    follow = turn is not None
    shape = (length, channels)
    outs = [(shape, jnp.bfloat16)]
    if follow:
        outs += [(shape, jnp.bfloat16)] * 2
    return call(
        lambda *refs: layer_kernel(*refs, spacing=spacing, offset=offset, follow=follow),
        "layer",
        [*pieces, active, layer_in] + ([turn] if follow else []),
        outs,
        [pltpu.VMEM((3 * channels, channels), jnp.bfloat16)],
        edges,
    )


def weight_kernel(active_ref, grad_ref, *outs, spacing, offset, halo, side):
    channels = active_ref.shape[1]
    length = grad_ref.shape[0] - 2 * halo
    half = channels // 2
    turned = active_ref[offset : offset + length, side * half : (side + 1) * half].T
    for tap in range(3):
        first = halo + (1 - tap) * spacing
        term = jnp.dot(
            turned, grad_ref[first : first + length], preferred_element_type=jnp.float32
        )
        if len(outs) == 3:
            outs[tap][...] = term.astype(jnp.bfloat16)
        else:
            outs[0][tap] = term


def weight_term(active, offset, grad_wide, side, spacing, halo):
    channels = active.shape[1]
    half = channels // 2
    if side == 0:
        outs = [((3, half, channels), jnp.float32)]
    else:
        outs = [((half, channels), jnp.bfloat16)] * 3
    out = call(
        lambda *refs: weight_kernel(*refs, spacing=spacing, offset=offset, halo=halo, side=side),
        "weight_term",
        [active, grad_wide],
        outs,
    )
    return out[0] if side == 0 else out


def pass_kernel(edge_ref, *refs, spacing, offset, unrolled):
    pieces, refs = refs[:4], refs[4:]
    grad_ref, grad_rel_ref, layer_in_ref, turn_ref, out_ref, rel_ref, weight, act_grad = refs
    length, channels = out_ref.shape
    size = channels // 4
    for tap in range(3):
        for index, piece in enumerate(pieces):
            weight[index * size : (index + 1) * size, tap * channels : (tap + 1) * channels] = piece[tap]

    def block(first, rows):
        windows = [grad_ref[span(first + (2 - tap) * spacing, rows)] for tap in range(3)]
        act_grad[...] = lax.dot_general(
            jnp.concatenate(windows, axis=1),
            weight[...],
            (((1,), (1,)), ((), ())),
            preferred_element_type=jnp.float32,
        )
        for start in range(0, rows, CHUNK):
            values = layer_in_ref[span(offset + first + start, CHUNK)].astype(jnp.float32)
            inv_rms = inverse_rms(values)
            normed = values * inv_rms
            slope = (
                cumulative_of(normed)
                + normed * jnp.exp(-0.5 * normed * normed) * 0.3989422804014327
            )
            norm_grad = act_grad[start : start + CHUNK] * slope
            passed = grad_rel_ref[span(first + start, CHUNK)].astype(jnp.float32) + inv_rms * (
                norm_grad - normed * jnp.mean(norm_grad * normed, axis=-1, keepdims=True)
            )
            passed = jnp.where(inside(edge_ref, first + start, CHUNK), passed, 0.0)
            rel_ref[start : start + CHUNK] = passed.astype(jnp.bfloat16)
        out_ref[span(first, rows)] = lax.dot_general(
            rel_ref[...], turn_ref[...], (((1,), (1,)), ((), ())), preferred_element_type=jnp.float32
        ).astype(jnp.bfloat16)

    over_blocks(length, block, unrolled)


def pass_down(edges, pieces, grad_pad, grad_rel, layer_in, offset, turn, spacing, unrolled):
    length = grad_pad.shape[0] - 2 * spacing
    channels = layer_in.shape[1]
    shape = (length, channels)
    return call(
        lambda *refs: pass_kernel(*refs, spacing=spacing, offset=offset, unrolled=unrolled),
        "pass_down",
        [*pieces, grad_pad, grad_rel, layer_in, turn],
        [(shape, jnp.bfloat16)],
        [
            pltpu.VMEM((length // BLOCKS, channels), jnp.bfloat16),
            pltpu.VMEM((channels, 3 * channels), jnp.bfloat16),
            pltpu.VMEM((length // BLOCKS, channels), jnp.float32),
        ],
        edges,
    )[0]


def per_device(inputs, weight_one, weight_two, cotangent):
    count = lax.axis_size("seq")
    me = lax.axis_index("seq")
    length, channels = inputs.shape
    grad_scale = 1.0 / math.sqrt(length * count)
    block = weight_one.shape[0]
    routes = routes_of(count)
    turn_one = one_hot(count, routes[0], block)
    turn_two = one_hot(count, routes[1], block)

    back_rows = length + 2 * DILATION_A
    hidden_rows = length + 2 * DILATION_B

    def edges_of(rows, halo):
        first = jnp.where(me > 0, 0, halo)
        last = jnp.where(me < count - 1, rows, rows - halo)
        return jnp.stack([first, last]).astype(jnp.int32)

    odd = (me & 1) == 1
    scalars = lax.optimization_barrier(
        (
            edges_of(hidden_rows, DILATION_B),
            edges_of(back_rows, DILATION_A),
            edges_of(length, 0),
            odd.astype(jnp.int32).reshape(1),
            turn_one,
            turn_two,
        )
    )
    hidden_edges, back_edges, own_edges, odd_flag, turn_one, turn_two = scalars

    one, two = Gather(weight_one, routes[0]), Gather(weight_two, routes[1])

    def gather_both(*others):
        joined = two.join(*others)
        joined = one.join(joined)
        one.send()
        two.send()
        return joined

    one.send()
    edges_low = jnp.concatenate([inputs[:HALO], cotangent[:HALO]])
    edges_high = jnp.concatenate([inputs[length - HALO :], cotangent[length - HALO :]])
    inner = jnp.where(odd, edges_low, edges_high)
    outer = jnp.where(odd, edges_high, edges_low)
    joined = one.join(inner, outer, *scalars)
    one.send()
    two.held = after(two.held, joined)
    two.send()
    across = [(i, i + 1) for i in range(1, count - 1, 2)] + [(i + 1, i) for i in range(1, count - 1, 2)]
    inner = lax.ppermute(after(inner, joined), "seq", core_pairs(count))
    outer = lax.ppermute(after(outer, joined), "seq", across)
    joined = one.join()
    one.send()
    joined = two.join(joined, inner, outer)
    two.send()
    for _ in range(one.steps - 3):
        joined = gather_both()
    wide_in, wide_cot, active_one, cot_rel = first_active(
        odd_flag, inputs, cotangent, inner, outer, turn_one, turn_two, DILATION_B, back_rows
    )
    joined = gather_both(cot_rel)
    full_one = one.full()

    hidden, rel_two, active_two = layer(
        hidden_edges,
        full_one,
        after(active_one, joined),
        wide_in,
        DILATION_A,
        hidden_rows,
        DILATION_A,
        turn_two,
    )
    send_two = weight_term(active_two, DILATION_B, wide_cot, 1, DILATION_B, HALO)
    scatter_two = Scatter(send_two, routes[1])
    joined = two.join(*send_two)
    two.send()
    full_two = two.full()
    scatter_two.keep(
        weight_term(active_two, DILATION_B, after(wide_cot, joined), 0, DILATION_B, HALO)
    )
    sent = scatter_two.add()

    wide_grad = pass_down(
        back_edges,
        full_two,
        after(wide_cot, sent),
        cot_rel,
        rel_two,
        DILATION_B - DILATION_A,
        turn_two,
        DILATION_B,
        True,
    )

    send_one = weight_term(active_one, HALO, wide_grad, 1, DILATION_A, DILATION_A)
    scatter_one = Scatter(send_one, routes[0])
    keep_one = weight_term(active_one, HALO, after(wide_grad, *send_one), 0, DILATION_A, DILATION_A)
    scatter_one.keep(keep_one)
    sent = scatter_two.add(keep_one)
    sent = scatter_one.add(sent)
    own_rel = permute_channels(after(wide_grad, sent)[DILATION_A : DILATION_A + length], turn_one, 0)
    input_grad = pass_down(
        own_edges,
        full_one,
        wide_grad,
        own_rel,
        permute_channels(after(inputs, sent), turn_one, 0),
        0,
        turn_one,
        DILATION_A,
        False,
    )
    sent = scatter_two.add(input_grad)
    sent = scatter_one.add(sent)
    (outputs,) = layer(
        own_edges,
        full_two,
        after(active_two, sent),
        hidden,
        DILATION_B,
        length,
        DILATION_B,
    )
    rest = [outputs]
    while scatter_one.left:
        if scatter_two.left:
            rest = [scatter_two.add(*rest)]
        rest = [scatter_one.add(*rest)]
    grad_one = scatter_one.finish(grad_scale)
    grad_two = scatter_two.finish(grad_scale)
    return (outputs, input_grad, grad_one, grad_two)


def solution(mesh):
    in_specs = (P("seq", None), P("seq", None, None), P("seq", None, None), P("seq", None))
    out_specs = (P("seq", None), P("seq", None), P("seq", None, None), P("seq", None, None))
    return jax.shard_map(
        per_device, mesh=mesh, in_specs=in_specs, out_specs=out_specs, check_vma=False
    )
```

profile of v0, /device:TPU:0, one launch (start us, length us, event | category | flops | bytes accessed | tf_op | source)
XLA Modules:
  0.0 116.6 jit_solution(4582075215215999258)
XLA Ops:
  0.6 4.1 %collective-permute-start = (bf16[3,24,768]{2,1,0:T(8,128)(2,1)}, bf16[3,24,768]{2,1,0:T(8,128)(2,1)S(1)}, u32[]{:S(2)}, u32[]{:S(2)}) collective-permute-start(bf16[3,24,768]{2,1,0:T(8,128)(2,1)} %bitcast.26), channel_id=1, source_target_pairs={{0,16},{1,17},{2,18},{3,19},{4,20},{5,21},{6,22},{7,23},{8,24},{9,... | collective-permute-start | bytes 331784 | tf_op jit(solution)/shard_map/ppermute | solution.py:69
  7.0 3.4 %collective-permute-done = bf16[3,24,768]{2,1,0:T(8,128)(2,1)S(1)} collective-permute-done((bf16[3,24,768]{2,1,0:T(8,128)(2,1)}, bf16[3,24,768]{2,1,0:T(8,128)(2,1)S(1)}, u32[]{:S(2)}, u32[]{:S(2)}) %collective-permute-start) | collective-permute-done | bytes 110624 | tf_op jit(solution)/shard_map/ppermute | solution.py:69
  12.0 2.9 %collective-permute-start.3 = (bf16[192,768]{1,0:T(8,128)(2,1)S(1)}, bf16[192,768]{1,0:T(8,128)(2,1)S(1)}, u32[]{:S(2)}, u32[]{:S(2)}) collective-permute-start(bf16[192,768]{1,0:T(8,128)(2,1)S(1)} %get-tuple-element.75), channel_id=1, source_target_pairs={{0,1},{1,0},{2,3},{3,2},{4,5},{5,4},{6,7},{7,6},{8,9},{9,8},{10,11... | collective-permute-start | bytes 884744 | tf_op jit(solution)/shard_map/ppermute | solution.py:428
  14.9 3.3 %collective-permute-start.1 = (bf16[3,24,768]{2,1,0:T(8,128)(2,1)S(1)}, bf16[3,24,768]{2,1,0:T(8,128)(2,1)S(1)}, u32[]{:S(2)}, u32[]{:S(2)}) collective-permute-start(bf16[3,24,768]{2,1,0:T(8,128)(2,1)S(1)} %bitcast.28), channel_id=1, source_target_pairs={{0,16},{1,17},{2,18},{3,19},{4,20},{5,21},{6,22},{7,23},{8,24},{9,... | collective-permute-start | bytes 331784 | tf_op jit(solution)/shard_map/ppermute | solution.py:69
  19.7 5.0 %collective-permute-done.1 = bf16[3,24,768]{2,1,0:T(8,128)(2,1)S(1)} collective-permute-done((bf16[3,24,768]{2,1,0:T(8,128)(2,1)S(1)}, bf16[3,24,768]{2,1,0:T(8,128)(2,1)S(1)}, u32[]{:S(2)}, u32[]{:S(2)}) %collective-permute-start.1) | collective-permute-done | bytes 110624 | tf_op jit(solution)/shard_map/ppermute | solution.py:69
  25.4 5.4 %collective-permute-done.5.second_ref = bf16[3,48,768]{2,1,0:T(8,128)(2,1)S(1)} collective-permute-done((bf16[3,48,768]{2,1,0:T(8,128)(2,1)S(1)}, bf16[3,48,768]{2,1,0:T(8,128)(2,1)S(1)}, u32[]{:S(2)}, u32[]{:S(2)}) %collective-permute-start.5) | collective-permute-done | bytes 221216 | tf_op jit(solution)/shard_map/ppermute | solution.py:69
  33.0 5.5 %first_active.1 = (bf16[1216,768]{1,0:T(8,128)(2,1)S(1)}, bf16[1216,768]{1,0:T(8,128)(2,1)S(1)}, bf16[1216,768]{1,0:T(8,128)(2,1)S(1)}, bf16[1088,768]{1,0:T(8,128)(2,1)S(1)}) custom-call(s32[1]{0:T(128)} %bitcast.4.refs_0_, bf16[1024,768]{1,0:T(8,128)(2,1)S(1)} %copy-done.1, bf16[1024,768]{1,0:T(8,128)(2,1)S(1)} %copy-done, ...), custom_call_target="tpu_custom_call" | custom-call | tf_op jit(solution)/shard_map/first_active/pallas_call | solution.py:131
  38.6 3.9 %collective-permute-done.6.second_ref = bf16[3,96,768]{2,1,0:T(8,128)(2,1)S(1)} collective-permute-done((bf16[3,96,768]{2,1,0:T(8,128)(2,1)S(1)}, bf16[3,96,768]{2,1,0:T(8,128)(2,1)S(1)}, u32[]{:S(2)}, u32[]{:S(2)}) %collective-permute-start.6) | collective-permute-done | bytes 442400 | tf_op jit(solution)/shard_map/ppermute | solution.py:69
  44.6 1.8 %collective-permute-done.11.refs_4_ = bf16[3,192,768]{2,1,0:T(8,128)(2,1)S(1)} collective-permute-done((bf16[3,192,768]{2,1,0:T(8,128)(2,1)S(1)}, bf16[3,192,768]{2,1,0:T(8,128)(2,1)S(1)}, u32[]{:S(2)}, u32[]{:S(2)}) %collective-permute-start.11) | collective-permute-done | bytes 884768 | tf_op jit(solution)/shard_map/ppermute | solution.py:71
  46.4 7.1 %layer.2 = (bf16[1152,768]{1,0:T(8,128)(2,1)S(1)}, bf16[1152,768]{1,0:T(8,128)(2,1)S(1)}, bf16[1152,768]{1,0:T(8,128)(2,1)S(1)}) custom-call(s32[2]{0:T(128)S(1)} %get-tuple-element.68.refs_0_, bf16[3,192,768]{2,1,0:T(8,128)(2,1)S(1)} %join_rows.7.refs_1_, bf16[3,192,768]{2,1,0:T(8,128)(2,1)S(1)} %collective-permute-done.9.refs_2_, ...), custom_call_target="tpu_custom_call" | custom-call | tf_op jit(solution)/shard_map/layer/pallas_call | solution.py:131
  53.5 2.0 %weight_term.4 = (bf16[384,768]{1,0:T(8,128)(2,1)S(1)}, bf16[384,768]{1,0:T(8,128)(2,1)S(1)}, bf16[384,768]{1,0:T(8,128)(2,1)S(1)}) custom-call(bf16[1152,768]{1,0:T(8,128)(2,1)S(1)} %get-tuple-element.117.refs_0_.refs_5_, bf16[1216,768]{1,0:T(8,128)(2,1)S(1)} %get-tuple-element.96.refs_1_.refs_5_), custom_call_target="tpu_custom_call" | custom-call | tf_op jit(solution)/shard_map/weight_term/pallas_call | solution.py:131
  57.0 2.0 %weight_term.5 = f32[3,384,768]{2,1,0:T(8,128)S(1)} custom-call(bf16[1152,768]{1,0:T(8,128)(2,1)S(1)} %get-tuple-element.117.refs_0_.refs_5_, bf16[1216,768]{1,0:T(8,128)(2,1)S(1)} %get-tuple-element.96.refs_1_.refs_5_), custom_call_target="tpu_custom_call" | custom-call | tf_op jit(solution)/shard_map/weight_term/pallas_call | solution.py:131
  61.9 7.8 %pass_down.2.refs_1_.refs_5_ = bf16[1088,768]{1,0:T(8,128)(2,1)S(1)} custom-call(s32[2]{0:T(128)S(1)} %get-tuple-element.69.refs_0_, bf16[3,192,768]{2,1,0:T(8,128)(2,1)S(1)} %join_rows.6.refs_1_, bf16[3,192,768]{2,1,0:T(8,128)(2,1)S(1)} %collective-permute-done.7.refs_2_, bf16[3,192,768]{2,1,0:T(8,128)(2,1)S(1)} %collective-permute-done.12.refs_3_, ...), custom_call_target="tpu_custom_call" | custom-call | tf_op jit(solution)/shard_map/pass_down/pallas_call | solution.py:131
  69.6 2.0 %weight_term.6 = (bf16[384,768]{1,0:T(8,128)(2,1)S(1)}, bf16[384,768]{1,0:T(8,128)(2,1)S(1)}, bf16[384,768]{1,0:T(8,128)(2,1)S(1)}) custom-call(bf16[1216,768]{1,0:T(8,128)(2,1)S(1)} %get-tuple-element.83.refs_5_.refs_0_, bf16[1088,768]{1,0:T(8,128)(2,1)S(1)} %pass_down.2.refs_1_.refs_5_), custom_call_target="tpu_custom_call" | custom-call | tf_op jit(solution)/shard_map/weight_term/pallas_call | solution.py:131
  72.4 2.0 %weight_term.7 = f32[3,384,768]{2,1,0:T(8,128)S(1)} custom-call(bf16[1216,768]{1,0:T(8,128)(2,1)S(1)} %get-tuple-element.83.refs_5_.refs_0_, bf16[1088,768]{1,0:T(8,128)(2,1)S(1)} %pass_down.2.refs_1_.refs_5_), custom_call_target="tpu_custom_call" | custom-call | tf_op jit(solution)/shard_map/weight_term/pallas_call | solution.py:131
  74.7 2.1 %collective-permute-start.22 = (bf16[3,96,768]{2,1,0:T(8,128)(2,1)S(1)}, bf16[3,96,768]{2,1,0:T(8,128)(2,1)S(1)}, u32[]{:S(2)}, u32[]{:S(2)}) collective-permute-start(bf16[3,96,768]{2,1,0:T(8,128)(2,1)S(1)} %get-tuple-element.104), channel_id=1, source_target_pairs={{0,8},{1,9},{2,10},{3,11},{4,12},{5,13},{6,14},{7,15},{8,0},{9,1},... | collective-permute-start | bytes 1327112 | tf_op jit(solution)/shard_map/ppermute | solution.py:107
  80.4 9.6 %pass_down.3 = bf16[1024,768]{1,0:T(8,128)(2,1)S(1)} custom-call(s32[2]{0:T(128)S(1)} %iota_multiply_fusion.refs_0_, bf16[3,192,768]{2,1,0:T(8,128)(2,1)S(1)} %join_rows.7.refs_1_, bf16[3,192,768]{2,1,0:T(8,128)(2,1)S(1)} %collective-permute-done.9.refs_2_, bf16[3,192,768]{2,1,0:T(8,128)(2,1)S(1)} %collective-permute-done.10.refs_3_, ...), custom_call_target="tpu_custom_call" | custom-call | tf_op jit(solution)/shard_map/pass_down/pallas_call | solution.py:131
  90.8 1.6 %collective-permute-start.23 = (bf16[3,96,768]{2,1,0:T(8,128)(2,1)S(1)}, bf16[3,96,768]{2,1,0:T(8,128)(2,1)S(1)}, u32[]{:S(2)}, u32[]{:S(2)}) collective-permute-start(bf16[3,96,768]{2,1,0:T(8,128)(2,1)S(1)} %get-tuple-element.116), channel_id=1, source_target_pairs={{0,2},{1,5},{2,0},{3,7},{4,6},{5,1},{6,4},{7,3},{8,10},{9,13},{10,... | collective-permute-start | bytes 1327112 | tf_op jit(solution)/shard_map/ppermute | solution.py:107
  92.4 5.1 %layer.3 = bf16[1024,768]{1,0:T(8,128)(2,1)S(1)} custom-call(s32[2]{0:T(128)S(1)} %iota_multiply_fusion.refs_0_, bf16[3,192,768]{2,1,0:T(8,128)(2,1)S(1)} %join_rows.6.refs_1_, bf16[3,192,768]{2,1,0:T(8,128)(2,1)S(1)} %collective-permute-done.7.refs_2_, bf16[3,192,768]{2,1,0:T(8,128)(2,1)S(1)} %collective-permute-done.12.refs_3_, ...), custom_call_target="tpu_custom_call" | custom-call | tf_op jit(solution)/shard_map/layer/pallas_call | solution.py:131
  97.6 3.2 %collective-permute-done.23 = bf16[3,96,768]{2,1,0:T(8,128)(2,1)S(1)} collective-permute-done((bf16[3,96,768]{2,1,0:T(8,128)(2,1)S(1)}, bf16[3,96,768]{2,1,0:T(8,128)(2,1)S(1)}, u32[]{:S(2)}, u32[]{:S(2)}) %collective-permute-start.23) | collective-permute-done | bytes 442400 | tf_op jit(solution)/shard_map/ppermute | solution.py:107
  102.9 2.8 %collective-permute-start.27 = (bf16[3,24,768]{2,1,0:T(8,128)(2,1)S(1)}, bf16[3,24,768]{2,1,0:T(8,128)(2,1)S(1)}, u32[]{:S(2)}, u32[]{:S(2)}) collective-permute-start(bf16[3,24,768]{2,1,0:T(8,128)(2,1)S(1)} %get-tuple-element.122), channel_id=1, source_target_pairs={{0,16},{1,17},{2,18},{3,19},{4,20},{5,21},{6,22},{7,23},{8,24},{9,... | collective-permute-start | bytes 331784 | tf_op jit(solution)/shard_map/ppermute | solution.py:107
  106.8 2.9 %collective-permute-done.25 = bf16[3,48,768]{2,1,0:T(8,128)(2,1)S(1)} collective-permute-done((bf16[3,48,768]{2,1,0:T(8,128)(2,1)S(1)}, bf16[3,48,768]{2,1,0:T(8,128)(2,1)S(1)}, u32[]{:S(2)}, u32[]{:S(2)}) %collective-permute-start.25) | collective-permute-done | bytes 221216 | tf_op jit(solution)/shard_map/ppermute | solution.py:107
  109.8 2.5 %collective-permute-start.26 = (bf16[3,24,768]{2,1,0:T(8,128)(2,1)S(1)}, bf16[3,24,768]{2,1,0:T(8,128)(2,1)S(1)}, u32[]{:S(2)}, u32[]{:S(2)}) collective-permute-start(bf16[3,24,768]{2,1,0:T(8,128)(2,1)S(1)} %get-tuple-element.128), channel_id=1, source_target_pairs={{0,16},{1,17},{2,18},{3,19},{4,20},{5,21},{6,22},{7,23},{8,24},{9,... | collective-permute-start | bytes 331784 | tf_op jit(solution)/shard_map/ppermute | solution.py:107
  113.1 2.8 %collective-permute-done.26 = bf16[3,24,768]{2,1,0:T(8,128)(2,1)S(1)} collective-permute-done((bf16[3,24,768]{2,1,0:T(8,128)(2,1)S(1)}, bf16[3,24,768]{2,1,0:T(8,128)(2,1)S(1)}, u32[]{:S(2)}, u32[]{:S(2)}) %collective-permute-start.26) | collective-permute-done | bytes 110624 | tf_op jit(solution)/shard_map/ppermute | solution.py:107
  (78 shorter events, 24.5 us)
Async XLA Ops:
  0.6 9.7 %collective-permute-start = (bf16[3,24,768]{2,1,0:T(8,128)(2,1)}, bf16[3,24,768]{2,1,0:T(8,128)(2,1)S(1)}, u32[]{:S(2)}, u32[]{:S(2)}) collective-permute-start(bf16[3,24,768]{2,1,0:T(8,128)(2,1)} %bitcast.26), channel_id=1, source_target_pairs={{0,16},{1,17},{2,18},{3,19},{4,20},{5,21},{6,22},{7,23},{8,24},{9,... | collective-permute-start | bytes 331784 | tf_op jit(solution)/shard_map/ppermute | solution.py:69
  10.4 7.7 %collective-permute-start.2 = (bf16[3,48,768]{2,1,0:T(8,128)(2,1)S(1)}, bf16[3,48,768]{2,1,0:T(8,128)(2,1)S(1)}, u32[]{:S(2)}, u32[]{:S(2)}) collective-permute-start(bf16[3,48,768]{2,1,0:T(8,128)(2,1)S(1)} %pad_maximum_fusion.4.first_ref), channel_id=1, source_target_pairs={{0,8},{1,9},{2,10},{3,11},{4,12},{5,13},{6,14},{7,15},{8,0},{9,1},... | collective-permute-start | bytes 663560 | tf_op jit(solution)/shard_map/ppermute | solution.py:69
  11.3 13.5 %collective-permute-start.4 = (bf16[192,768]{1,0:T(8,128)(2,1)S(1)}, bf16[192,768]{1,0:T(8,128)(2,1)S(1)}, u32[]{:S(2)}, u32[]{:S(2)}) collective-permute-start(bf16[192,768]{1,0:T(8,128)(2,1)S(1)} %get-tuple-element.76), channel_id=1, source_target_pairs={{1,2},{3,4},{5,6},{7,8},{9,10},{11,12},{13,14},{15,16},{17,18},{19... | collective-permute-start | bytes 884744 | tf_op jit(solution)/shard_map/ppermute | solution.py:429
  12.0 12.8 %collective-permute-start.3 = (bf16[192,768]{1,0:T(8,128)(2,1)S(1)}, bf16[192,768]{1,0:T(8,128)(2,1)S(1)}, u32[]{:S(2)}, u32[]{:S(2)}) collective-permute-start(bf16[192,768]{1,0:T(8,128)(2,1)S(1)} %get-tuple-element.75), channel_id=1, source_target_pairs={{0,1},{1,0},{2,3},{3,2},{4,5},{5,4},{6,7},{7,6},{8,9},{9,8},{10,11... | collective-permute-start | bytes 884744 | tf_op jit(solution)/shard_map/ppermute | solution.py:428
  14.9 9.9 %collective-permute-start.1 = (bf16[3,24,768]{2,1,0:T(8,128)(2,1)S(1)}, bf16[3,24,768]{2,1,0:T(8,128)(2,1)S(1)}, u32[]{:S(2)}, u32[]{:S(2)}) collective-permute-start(bf16[3,24,768]{2,1,0:T(8,128)(2,1)S(1)} %bitcast.28), channel_id=1, source_target_pairs={{0,16},{1,17},{2,18},{3,19},{4,20},{5,21},{6,22},{7,23},{8,24},{9,... | collective-permute-start | bytes 331784 | tf_op jit(solution)/shard_map/ppermute | solution.py:69
  18.2 12.6 %collective-permute-start.8 = (bf16[3,96,768]{2,1,0:T(8,128)(2,1)S(1)}, bf16[3,96,768]{2,1,0:T(8,128)(2,1)S(1)}, u32[]{:S(2)}, u32[]{:S(2)}) collective-permute-start(bf16[3,96,768]{2,1,0:T(8,128)(2,1)S(1)} %join_rows.4.first_ref), channel_id=1, source_target_pairs={{0,2},{1,5},{2,0},{3,7},{4,6},{5,1},{6,4},{7,3},{8,10},{9,13},{10,... | collective-permute-start | bytes 1327112 | tf_op jit(solution)/shard_map/ppermute | solution.py:69
  24.8 6.0 %collective-permute-start.5 = (bf16[3,48,768]{2,1,0:T(8,128)(2,1)S(1)}, bf16[3,48,768]{2,1,0:T(8,128)(2,1)S(1)}, u32[]{:S(2)}, u32[]{:S(2)}) collective-permute-start(bf16[3,48,768]{2,1,0:T(8,128)(2,1)S(1)} %pad_maximum_fusion.5.first_ref), channel_id=1, source_target_pairs={{0,2},{1,5},{2,0},{3,7},{4,6},{5,1},{6,4},{7,3},{8,10},{9,13},{10,... | collective-permute-start | bytes 663560 | tf_op jit(solution)/shard_map/ppermute | solution.py:69
  30.9 13.1 %collective-permute-start.9 = (bf16[3,192,768]{2,1,0:T(8,128)(2,1)S(1)}, bf16[3,192,768]{2,1,0:T(8,128)(2,1)S(1)}, u32[]{:S(2)}, u32[]{:S(2)}) collective-permute-start(bf16[3,192,768]{2,1,0:T(8,128)(2,1)S(1)} %join_rows.7.refs_1_), channel_id=1, source_target_pairs={{0,4},{1,3},{2,6},{3,1},{4,0},{5,7},{6,2},{7,5},{8,12},{9,11},{10,... | collective-permute-start | bytes 2654216 | tf_op jit(solution)/shard_map/ppermute | solution.py:69
  31.5 11.0 %collective-permute-start.6 = (bf16[3,96,768]{2,1,0:T(8,128)(2,1)S(1)}, bf16[3,96,768]{2,1,0:T(8,128)(2,1)S(1)}, u32[]{:S(2)}, u32[]{:S(2)}) collective-permute-start(bf16[3,96,768]{2,1,0:T(8,128)(2,1)S(1)} %join_rows.5.first_ref), channel_id=1, source_target_pairs={{0,8},{1,9},{2,10},{3,11},{4,12},{5,13},{6,14},{7,15},{8,0},{9,1},... | collective-permute-start | bytes 1327112 | tf_op jit(solution)/shard_map/ppermute | solution.py:69
  38.6 6.0 %collective-permute-start.10 = (bf16[3,192,768]{2,1,0:T(8,128)(2,1)S(1)}, bf16[3,192,768]{2,1,0:T(8,128)(2,1)S(1)}, u32[]{:S(2)}, u32[]{:S(2)}) collective-permute-start(bf16[3,192,768]{2,1,0:T(8,128)(2,1)S(1)} %join_rows.7.refs_1_), channel_id=1, source_target_pairs={{0,1},{1,0},{2,3},{3,2},{4,5},{5,4},{6,7},{7,6},{8,9},{9,8},{10,11... | collective-permute-start | bytes 2654216 | tf_op jit(solution)/shard_map/ppermute | solution.py:71
  44.0 13.0 %collective-permute-start.7 = (bf16[3,192,768]{2,1,0:T(8,128)(2,1)S(1)}, bf16[3,192,768]{2,1,0:T(8,128)(2,1)S(1)}, u32[]{:S(2)}, u32[]{:S(2)}) collective-permute-start(bf16[3,192,768]{2,1,0:T(8,128)(2,1)S(1)} %join_rows.6.refs_1_), channel_id=1, source_target_pairs={{0,4},{1,3},{2,6},{3,1},{4,0},{5,7},{6,2},{7,5},{8,12},{9,11},{10,... | collective-permute-start | bytes 2654216 | tf_op jit(solution)/shard_map/ppermute | solution.py:69
  56.3 4.4 %collective-permute-start.12 = (bf16[3,192,768]{2,1,0:T(8,128)(2,1)S(1)}, bf16[3,192,768]{2,1,0:T(8,128)(2,1)S(1)}, u32[]{:S(2)}, u32[]{:S(2)}) collective-permute-start(bf16[3,192,768]{2,1,0:T(8,128)(2,1)S(1)} %join_rows.6.refs_1_), channel_id=1, source_target_pairs={{0,1},{1,0},{2,3},{3,2},{4,5},{5,4},{6,7},{7,6},{8,9},{9,8},{10,11... | collective-permute-start | bytes 2654216 | tf_op jit(solution)/shard_map/ppermute | solution.py:71
  57.0 4.8 %collective-permute-start.13 = (bf16[3,192,768]{2,1,0:T(8,128)(2,1)S(1)}, bf16[3,192,768]{2,1,0:T(8,128)(2,1)S(1)}, u32[]{:S(2)}, u32[]{:S(2)}) collective-permute-start(bf16[3,192,768]{2,1,0:T(8,128)(2,1)S(1)} %collective-permute-done.7.refs_2_), channel_id=1, source_target_pairs={{0,1},{1,0},{2,3},{3,2},{4,5},{5,4},{6,7},{7,6},{8,9},{9,8},{10,11... | collective-permute-start | bytes 2654216 | tf_op jit(solution)/shard_map/ppermute | solution.py:71
  60.0 14.5 %collective-permute-start.20 = (bf16[3,192,768]{2,1,0:T(8,128)(2,1)S(1)}, bf16[3,192,768]{2,1,0:T(8,128)(2,1)S(1)}, u32[]{:S(2)}, u32[]{:S(2)}) collective-permute-start(bf16[3,192,768]{2,1,0:T(8,128)(2,1)S(1)} %get-tuple-element.95), channel_id=1, source_target_pairs={{0,4},{1,3},{2,6},{3,1},{4,0},{5,7},{6,2},{7,5},{8,12},{9,11},{10,... | collective-permute-start | bytes 2654216 | tf_op jit(solution)/shard_map/ppermute | solution.py:107
  71.7 5.1 %collective-permute-start.17 = (bf16[384,768]{1,0:T(8,128)(2,1)S(1)}, bf16[384,768]{1,0:T(8,128)(2,1)S(1)}, u32[]{:S(2)}, u32[]{:S(2)}) collective-permute-start(bf16[384,768]{1,0:T(8,128)(2,1)S(1)} %get-tuple-element.98), channel_id=1, source_target_pairs={{0,1},{1,0},{2,3},{3,2},{4,5},{5,4},{6,7},{7,6},{8,9},{9,8},{10,11... | collective-permute-start | bytes 1769480 | tf_op jit(solution)/shard_map/ppermute | solution.py:91
  71.9 4.9 %collective-permute-start.18 = (bf16[384,768]{1,0:T(8,128)(2,1)S(1)}, bf16[384,768]{1,0:T(8,128)(2,1)S(1)}, u32[]{:S(2)}, u32[]{:S(2)}) collective-permute-start(bf16[384,768]{1,0:T(8,128)(2,1)S(1)} %get-tuple-element.99), channel_id=1, source_target_pairs={{0,1},{1,0},{2,3},{3,2},{4,5},{5,4},{6,7},{7,6},{8,9},{9,8},{10,11... | collective-permute-start | bytes 1769480 | tf_op jit(solution)/shard_map/ppermute | solution.py:91
  72.3 4.5 %collective-permute-start.19 = (bf16[384,768]{1,0:T(8,128)(2,1)S(1)}, bf16[384,768]{1,0:T(8,128)(2,1)S(1)}, u32[]{:S(2)}, u32[]{:S(2)}) collective-permute-start(bf16[384,768]{1,0:T(8,128)(2,1)S(1)} %get-tuple-element.100), channel_id=1, source_target_pairs={{0,1},{1,0},{2,3},{3,2},{4,5},{5,4},{6,7},{7,6},{8,9},{9,8},{10,11... | collective-permute-start | bytes 1769480 | tf_op jit(solution)/shard_map/ppermute | solution.py:91
  74.7 15.3 %collective-permute-start.22 = (bf16[3,96,768]{2,1,0:T(8,128)(2,1)S(1)}, bf16[3,96,768]{2,1,0:T(8,128)(2,1)S(1)}, u32[]{:S(2)}, u32[]{:S(2)}) collective-permute-start(bf16[3,96,768]{2,1,0:T(8,128)(2,1)S(1)} %get-tuple-element.104), channel_id=1, source_target_pairs={{0,8},{1,9},{2,10},{3,11},{4,12},{5,13},{6,14},{7,15},{8,0},{9,1},... | collective-permute-start | bytes 1327112 | tf_op jit(solution)/shard_map/ppermute | solution.py:107
  77.4 13.3 %collective-permute-start.21 = (bf16[3,192,768]{2,1,0:T(8,128)(2,1)S(1)}, bf16[3,192,768]{2,1,0:T(8,128)(2,1)S(1)}, u32[]{:S(2)}, u32[]{:S(2)}) collective-permute-start(bf16[3,192,768]{2,1,0:T(8,128)(2,1)S(1)} %get-tuple-element.109), channel_id=1, source_target_pairs={{0,4},{1,3},{2,6},{3,1},{4,0},{5,7},{6,2},{7,5},{8,12},{9,11},{10,... | collective-permute-start | bytes 2654216 | tf_op jit(solution)/shard_map/ppermute | solution.py:107
  90.1 7.5 %collective-permute-start.24 = (bf16[3,48,768]{2,1,0:T(8,128)(2,1)S(1)}, bf16[3,48,768]{2,1,0:T(8,128)(2,1)S(1)}, u32[]{:S(2)}, u32[]{:S(2)}) collective-permute-start(bf16[3,48,768]{2,1,0:T(8,128)(2,1)S(1)} %get-tuple-element.114), channel_id=1, source_target_pairs={{0,2},{1,5},{2,0},{3,7},{4,6},{5,1},{6,4},{7,3},{8,10},{9,13},{10,... | collective-permute-start | bytes 663560 | tf_op jit(solution)/shard_map/ppermute | solution.py:107
  90.8 10.0 %collective-permute-start.23 = (bf16[3,96,768]{2,1,0:T(8,128)(2,1)S(1)}, bf16[3,96,768]{2,1,0:T(8,128)(2,1)S(1)}, u32[]{:S(2)}, u32[]{:S(2)}) collective-permute-start(bf16[3,96,768]{2,1,0:T(8,128)(2,1)S(1)} %get-tuple-element.116), channel_id=1, source_target_pairs={{0,2},{1,5},{2,0},{3,7},{4,6},{5,1},{6,4},{7,3},{8,10},{9,13},{10,... | collective-permute-start | bytes 1327112 | tf_op jit(solution)/shard_map/ppermute | solution.py:107
  100.9 8.9 %collective-permute-start.25 = (bf16[3,48,768]{2,1,0:T(8,128)(2,1)S(1)}, bf16[3,48,768]{2,1,0:T(8,128)(2,1)S(1)}, u32[]{:S(2)}, u32[]{:S(2)}) collective-permute-start(bf16[3,48,768]{2,1,0:T(8,128)(2,1)S(1)} %get-tuple-element.125), channel_id=1, source_target_pairs={{0,8},{1,9},{2,10},{3,11},{4,12},{5,13},{6,14},{7,15},{8,0},{9,1},... | collective-permute-start | bytes 663560 | tf_op jit(solution)/shard_map/ppermute | solution.py:107
  102.9 9.5 %collective-permute-start.27 = (bf16[3,24,768]{2,1,0:T(8,128)(2,1)S(1)}, bf16[3,24,768]{2,1,0:T(8,128)(2,1)S(1)}, u32[]{:S(2)}, u32[]{:S(2)}) collective-permute-start(bf16[3,24,768]{2,1,0:T(8,128)(2,1)S(1)} %get-tuple-element.122), channel_id=1, source_target_pairs={{0,16},{1,17},{2,18},{3,19},{4,20},{5,21},{6,22},{7,23},{8,24},{9,... | collective-permute-start | bytes 331784 | tf_op jit(solution)/shard_map/ppermute | solution.py:107
  109.8 6.1 %collective-permute-start.26 = (bf16[3,24,768]{2,1,0:T(8,128)(2,1)S(1)}, bf16[3,24,768]{2,1,0:T(8,128)(2,1)S(1)}, u32[]{:S(2)}, u32[]{:S(2)}) collective-permute-start(bf16[3,24,768]{2,1,0:T(8,128)(2,1)S(1)} %get-tuple-element.128), channel_id=1, source_target_pairs={{0,16},{1,17},{2,18},{3,19},{4,20},{5,21},{6,22},{7,23},{8,24},{9,... | collective-permute-start | bytes 331784 | tf_op jit(solution)/shard_map/ppermute | solution.py:107
  (8 other events, 57.0 us)
where the time goes:
time: 117 us
  Pallas kernels  43.5 us (37%)
  waiting for transfers between devices  31.7 us (27%)
  starting transfers between devices  29.8 us (25%)
  other arithmetic  4.39 us (4%)
  local copies, waits for them, and re-layouts  3.47 us (3%)
  matrix products  2.78 us (2%)
    pallas_call x13, Pallas kernels, call(): pl.pallas_call(kernel, in_specs=[pl.BlockSpec(memory_space=pltpu.SMEM)] *...  43.5 us
    ppermute x8, waiting for transfers between devices, send(): lax.ppermute(self.held, 'seq', step_pairs(count, self.route, self.step))  19.4 us
    ppermute x8, starting transfers between devices, send(): lax.ppermute(self.held, 'seq', step_pairs(count, self.route, self.step))  13.1 us
    ppermute x8, starting transfers between devices, add(): self.arrived = lax.ppermute(send, 'seq', pairs)  11.2 us
    ppermute x8, waiting for transfers between devices, add(): self.arrived = lax.ppermute(send, 'seq', pairs)  9.02 us
    ppermute x4, waiting for transfers between devices, send(): lax.ppermute(self.held, 'seq', core_pairs(count))  3.06 us
    ppermute x1, starting transfers between devices, per_device(): inner = lax.ppermute(after(inner, joined), 'seq', core_pairs(count))  2.9 us
    dot_general x2, matrix products, permute_channels(): lax.dot_general(values, matrix, (((1,), (dim,)), ((), ())), preferred_ele...  2.78 us
  transfers between devices with their start and end apart: 28, of which 12 were waited for; matrix products, arithmetic and copies ran while one was open for 8% of the time, Pallas kernels for 37%

commit v1 on v0

--- a/solution.py
+++ b/solution.py
@@ -94,6 +94,9 @@
         self.kept = keep
 
     def add(self, *others):
+        return self.go(self.total(*others))
+
+    def total(self, *others):
         arrived = self.arrived
         if isinstance(arrived, list):
             arrived = jnp.stack(lax.optimization_barrier(tuple(arrived) + others)[:3])
@@ -103,18 +106,17 @@
         send = (self.kept[:, half:] + arrived[:, half:].astype(jnp.float32)).astype(jnp.bfloat16)
         keep = self.kept[:, :half] + arrived[:, :half].astype(jnp.float32)
         send, self.kept = lax.optimization_barrier((send, keep))
+        return send
+
+    def go(self, send, *others):
+        if others:
+            send = after(send, *others)
         pairs = step_pairs(lax.axis_size("seq"), self.route, self.left.pop(0))
         self.arrived = lax.ppermute(send, "seq", pairs)
         return send
 
     def finish(self, grad_scale):
         return jnp.transpose((self.kept + self.arrived.astype(jnp.float32)) * grad_scale, (1, 0, 2))
-
-
-def permute_channels(values, matrix, dim):
-    return lax.dot_general(
-        values, matrix, (((1,), (dim,)), ((), ())), preferred_element_type=jnp.float32
-    ).astype(jnp.bfloat16)
 
 
 CHUNK = 16
@@ -195,7 +197,7 @@
 
 def active_kernel(
     odd_ref, layer_in_ref, grad_ref, inner_ref, outer_ref, turn_ref, next_turn_ref,
-    wide_in_ref, wide_grad_ref, active_ref, grad_rel_ref, rel_ref, *, offset
+    wide_in_ref, wide_grad_ref, active_ref, rel_ref, grad_rel_ref, *, offset
 ):
     length = layer_in_ref.shape[0]
     halo = inner_ref.shape[0] // 2
@@ -207,10 +209,10 @@
         wide_ref[halo + length :] = jnp.where(odd, outer_ref[rows], inner_ref[rows])
 
     def own_block(first, rows):
-        rel_ref[...] = jnp.dot(
+        rel_ref[span(first, rows)] = jnp.dot(
             wide_in_ref[span(first, rows)], turn_ref[...], preferred_element_type=jnp.float32
         ).astype(jnp.bfloat16)
-        activate(first, rel_ref, active_ref)
+        activate(first, rel_ref.at[span(first, rows)], active_ref)
 
     def grad_block(first, rows):
         grad_rel_ref[span(first, rows)] = jnp.dot(
@@ -231,8 +233,8 @@
         lambda *refs: active_kernel(*refs, offset=offset),
         "first_active",
         [layer_in, grad, inner, outer, turn, next_turn],
-        [wide, wide, wide, ((back_rows, channels), jnp.bfloat16)],
-        [pltpu.VMEM((rows // BLOCKS, channels), jnp.bfloat16)],
+        [wide, wide, wide, wide, ((back_rows, channels), jnp.bfloat16)],
+        (),
         odd,
         room=6,
     )
@@ -321,7 +323,8 @@
 
 def pass_kernel(edge_ref, *refs, spacing, offset, unrolled):
     pieces, refs = refs[:4], refs[4:]
-    grad_ref, grad_rel_ref, layer_in_ref, turn_ref, out_ref, rel_ref, weight, act_grad = refs
+    grad_ref, layer_in_ref, turn_ref, *refs = refs
+    grad_rel_ref, out_ref, rel_ref, weight, act_grad = refs if unrolled else refs[-1:] + refs[:-1]
     length, channels = out_ref.shape
     size = channels // 4
     for tap in range(3):
@@ -336,6 +339,10 @@
             (((1,), (1,)), ((), ())),
             preferred_element_type=jnp.float32,
         )
+        if not unrolled:
+            grad_rel_ref[...] = jnp.dot(
+                grad_ref[span(first + spacing, rows)], turn_ref[...], preferred_element_type=jnp.float32
+            ).astype(jnp.bfloat16)
         for start in range(0, rows, CHUNK):
             values = layer_in_ref[span(offset + first + start, CHUNK)].astype(jnp.float32)
             inv_rms = inverse_rms(values)
@@ -345,7 +352,7 @@
                 + normed * jnp.exp(-0.5 * normed * normed) * 0.3989422804014327
             )
             norm_grad = act_grad[start : start + CHUNK] * slope
-            passed = grad_rel_ref[span(first + start, CHUNK)].astype(jnp.float32) + inv_rms * (
+            passed = grad_rel_ref[span(first + start if unrolled else start, CHUNK)].astype(jnp.float32) + inv_rms * (
                 norm_grad - normed * jnp.mean(norm_grad * normed, axis=-1, keepdims=True)
             )
             passed = jnp.where(inside(edge_ref, first + start, CHUNK), passed, 0.0)
@@ -357,20 +364,22 @@
     over_blocks(length, block, unrolled)
 
 
-def pass_down(edges, pieces, grad_pad, grad_rel, layer_in, offset, turn, spacing, unrolled):
+def pass_down(edges, pieces, grad_pad, layer_in, offset, turn, spacing, grad_rel=None):
     length = grad_pad.shape[0] - 2 * spacing
     channels = layer_in.shape[1]
+    unrolled = grad_rel is not None
     shape = (length, channels)
     return call(
         lambda *refs: pass_kernel(*refs, spacing=spacing, offset=offset, unrolled=unrolled),
         "pass_down",
-        [*pieces, grad_pad, grad_rel, layer_in, turn],
+        [*pieces, grad_pad, layer_in, turn] + ([grad_rel] if unrolled else []),
         [(shape, jnp.bfloat16)],
         [
             pltpu.VMEM((length // BLOCKS, channels), jnp.bfloat16),
             pltpu.VMEM((channels, 3 * channels), jnp.bfloat16),
             pltpu.VMEM((length // BLOCKS, channels), jnp.float32),
-        ],
+        ]
+        + [pltpu.VMEM((length // BLOCKS, channels), jnp.bfloat16)] * (not unrolled),
         edges,
     )[0]
 
@@ -433,7 +442,7 @@
     two.send()
     for _ in range(one.steps - 3):
         joined = gather_both()
-    wide_in, wide_cot, active_one, cot_rel = first_active(
+    wide_in, wide_cot, active_one, rel_one, cot_rel = first_active(
         odd_flag, inputs, cotangent, inner, outer, turn_one, turn_two, DILATION_B, back_rows
     )
     joined = gather_both(cot_rel)
@@ -463,31 +472,28 @@
         back_edges,
         full_two,
         after(wide_cot, sent),
-        cot_rel,
         rel_two,
         DILATION_B - DILATION_A,
         turn_two,
         DILATION_B,
-        True,
+        cot_rel,
     )
 
     send_one = weight_term(active_one, HALO, wide_grad, 1, DILATION_A, DILATION_A)
     scatter_one = Scatter(send_one, routes[0])
     keep_one = weight_term(active_one, HALO, after(wide_grad, *send_one), 0, DILATION_A, DILATION_A)
     scatter_one.keep(keep_one)
-    sent = scatter_two.add(keep_one)
-    sent = scatter_one.add(sent)
-    own_rel = permute_channels(after(wide_grad, sent)[DILATION_A : DILATION_A + length], turn_one, 0)
+    send = scatter_two.total(keep_one)
+    sent = scatter_one.add(send)
+    sent = scatter_two.go(send, sent)
     input_grad = pass_down(
         own_edges,
         full_one,
-        wide_grad,
-        own_rel,
-        permute_channels(after(inputs, sent), turn_one, 0),
-        0,
+        after(wide_grad, sent),
+        rel_one,
+        HALO,
         turn_one,
         DILATION_A,
-        False,
     )
     sent = scatter_two.add(input_grad)
     sent = scatter_one.add(sent)

time: 117 us -> 115 us (0.983)
  matrix products: 2.78 us -> 0 us
  starting transfers between devices: 29.8 us -> 31.2 us
    dot_general x2 -> x0, matrix products: 2.78 us -> none  [permute_channels(): lax.dot_general(values, matrix, (((1,), (dim,)), ((), ())), preferred_ele...]
    ppermute x8, starting transfers between devices: 11.2 us -> 12.6 us  [go(): self.arrived = lax.ppermute(send, 'seq', pairs)]
  transfers between devices with their start and end apart: 28 -> 28, of which waited for: 12 -> 14; matrix products, arithmetic and copies ran while one was open for 8% -> 6% of each run, Pallas kernels for 37% -> 37%
where the time goes in v1:
time: 115 us
  Pallas kernels  42.5 us (37%)
  waiting for transfers between devices  32.8 us (29%)
  starting transfers between devices  31.2 us (27%)
  other arithmetic  4.4 us (4%)
  local copies, waits for them, and re-layouts  3.47 us (3%)
    pallas_call x13, Pallas kernels, call(): pl.pallas_call(kernel, in_specs=[pl.BlockSpec(memory_space=pltpu.SMEM)] *...  42.5 us
    ppermute x8, waiting for transfers between devices, send(): lax.ppermute(self.held, 'seq', step_pairs(count, self.route, self.step))  19.5 us
    ppermute x8, starting transfers between devices, send(): lax.ppermute(self.held, 'seq', step_pairs(count, self.route, self.step))  13.1 us
    ppermute x8, starting transfers between devices, go(): self.arrived = lax.ppermute(send, 'seq', pairs)  12.6 us
    ppermute x8, waiting for transfers between devices, go(): self.arrived = lax.ppermute(send, 'seq', pairs)  9.37 us
    ppermute x4, waiting for transfers between devices, send(): lax.ppermute(self.held, 'seq', core_pairs(count))  3.06 us
    ppermute x1, starting transfers between devices, per_device(): inner = lax.ppermute(after(inner, joined), 'seq', core_pairs(count))  2.9 us
    unnamed x10, local copies, waits for them, and re-layouts  2.31 us
  transfers between devices with their start and end apart: 28, of which 14 were waited for; matrix products, arithmetic and copies ran while one was open for 6% of the time, Pallas kernels for 37%

profile of v1, /device:TPU:0, one launch (start us, length us, event | category | flops | bytes accessed | tf_op | source)
XLA Modules:
  0.0 115.3 jit_solution(10329289402621237534)
XLA Ops:
  0.6 4.1 %collective-permute-start = (bf16[3,24,768]{2,1,0:T(8,128)(2,1)}, bf16[3,24,768]{2,1,0:T(8,128)(2,1)S(1)}, u32[]{:S(2)}, u32[]{:S(2)}) collective-permute-start(bf16[3,24,768]{2,1,0:T(8,128)(2,1)} %bitcast.23), channel_id=1, source_target_pairs={{0,16},{1,17},{2,18},{3,19},{4,20},{5,21},{6,22},{7,23},{8,24},{9,... | collective-permute-start | bytes 331784 | tf_op jit(solution)/shard_map/ppermute | solution.py:69
  7.0 3.4 %collective-permute-done = bf16[3,24,768]{2,1,0:T(8,128)(2,1)S(1)} collective-permute-done((bf16[3,24,768]{2,1,0:T(8,128)(2,1)}, bf16[3,24,768]{2,1,0:T(8,128)(2,1)S(1)}, u32[]{:S(2)}, u32[]{:S(2)}) %collective-permute-start) | collective-permute-done | bytes 110624 | tf_op jit(solution)/shard_map/ppermute | solution.py:69
  12.0 2.9 %collective-permute-start.3 = (bf16[192,768]{1,0:T(8,128)(2,1)S(1)}, bf16[192,768]{1,0:T(8,128)(2,1)S(1)}, u32[]{:S(2)}, u32[]{:S(2)}) collective-permute-start(bf16[192,768]{1,0:T(8,128)(2,1)S(1)} %get-tuple-element.76), channel_id=1, source_target_pairs={{0,1},{1,0},{2,3},{3,2},{4,5},{5,4},{6,7},{7,6},{8,9},{9,8},{10,11... | collective-permute-start | bytes 884744 | tf_op jit(solution)/shard_map/ppermute | solution.py:437
  14.9 3.3 %collective-permute-start.1 = (bf16[3,24,768]{2,1,0:T(8,128)(2,1)S(1)}, bf16[3,24,768]{2,1,0:T(8,128)(2,1)S(1)}, u32[]{:S(2)}, u32[]{:S(2)}) collective-permute-start(bf16[3,24,768]{2,1,0:T(8,128)(2,1)S(1)} %bitcast.25), channel_id=1, source_target_pairs={{0,16},{1,17},{2,18},{3,19},{4,20},{5,21},{6,22},{7,23},{8,24},{9,... | collective-permute-start | bytes 331784 | tf_op jit(solution)/shard_map/ppermute | solution.py:69
  19.7 5.0 %collective-permute-done.1 = bf16[3,24,768]{2,1,0:T(8,128)(2,1)S(1)} collective-permute-done((bf16[3,24,768]{2,1,0:T(8,128)(2,1)S(1)}, bf16[3,24,768]{2,1,0:T(8,128)(2,1)S(1)}, u32[]{:S(2)}, u32[]{:S(2)}) %collective-permute-start.1) | collective-permute-done | bytes 110624 | tf_op jit(solution)/shard_map/ppermute | solution.py:69
  25.4 5.4 %collective-permute-done.5.second_ref = bf16[3,48,768]{2,1,0:T(8,128)(2,1)S(1)} collective-permute-done((bf16[3,48,768]{2,1,0:T(8,128)(2,1)S(1)}, bf16[3,48,768]{2,1,0:T(8,128)(2,1)S(1)}, u32[]{:S(2)}, u32[]{:S(2)}) %collective-permute-start.5) | collective-permute-done | bytes 221216 | tf_op jit(solution)/shard_map/ppermute | solution.py:69
  33.0 5.5 %first_active.1 = (bf16[1216,768]{1,0:T(8,128)(2,1)S(1)}, bf16[1216,768]{1,0:T(8,128)(2,1)S(1)}, bf16[1216,768]{1,0:T(8,128)(2,1)S(1)}, bf16[1216,768]{1,0:T(8,128)(2,1)S(1)}, bf16[1088,768]{1,0:T(8,128)(2,1)S(1)}) custom-call(s32[1]{0:T(128)} %bitcast.4.refs_0_, bf16[1024,768]{1,0:T(8,128)(2,1)S(1)} %copy-done, bf16[1024,768]{1,0:T(8,128)(2,1)S(1)} %copy-done.1, ...), custom_call_target="tpu_custom_call" | custom-call | tf_op jit(solution)/shard_map/first_active/pallas_call | solution.py:133
  38.6 4.0 %collective-permute-done.6.second_ref = bf16[3,96,768]{2,1,0:T(8,128)(2,1)S(1)} collective-permute-done((bf16[3,96,768]{2,1,0:T(8,128)(2,1)S(1)}, bf16[3,96,768]{2,1,0:T(8,128)(2,1)S(1)}, u32[]{:S(2)}, u32[]{:S(2)}) %collective-permute-start.6) | collective-permute-done | bytes 442400 | tf_op jit(solution)/shard_map/ppermute | solution.py:69
  44.6 1.8 %collective-permute-done.11.refs_4_ = bf16[3,192,768]{2,1,0:T(8,128)(2,1)S(1)} collective-permute-done((bf16[3,192,768]{2,1,0:T(8,128)(2,1)S(1)}, bf16[3,192,768]{2,1,0:T(8,128)(2,1)S(1)}, u32[]{:S(2)}, u32[]{:S(2)}) %collective-permute-start.11) | collective-permute-done | bytes 884768 | tf_op jit(solution)/shard_map/ppermute | solution.py:71
  46.4 7.1 %layer.2 = (bf16[1152,768]{1,0:T(8,128)(2,1)S(1)}, bf16[1152,768]{1,0:T(8,128)(2,1)S(1)}, bf16[1152,768]{1,0:T(8,128)(2,1)S(1)}) custom-call(s32[2]{0:T(128)S(1)} %get-tuple-element.69.refs_0_, bf16[3,192,768]{2,1,0:T(8,128)(2,1)S(1)} %join_rows.7.refs_1_, bf16[3,192,768]{2,1,0:T(8,128)(2,1)S(1)} %collective-permute-done.9.refs_2_, ...), custom_call_target="tpu_custom_call" | custom-call | tf_op jit(solution)/shard_map/layer/pallas_call | solution.py:133
  53.5 2.0 %weight_term.4 = (bf16[384,768]{1,0:T(8,128)(2,1)S(1)}, bf16[384,768]{1,0:T(8,128)(2,1)S(1)}, bf16[384,768]{1,0:T(8,128)(2,1)S(1)}) custom-call(bf16[1152,768]{1,0:T(8,128)(2,1)S(1)} %get-tuple-element.119.refs_0_.refs_5_, bf16[1216,768]{1,0:T(8,128)(2,1)S(1)} %get-tuple-element.97.refs_1_.refs_5_), custom_call_target="tpu_custom_call" | custom-call | tf_op jit(solution)/shard_map/weight_term/pallas_call | solution.py:133
  57.0 2.0 %weight_term.5 = f32[3,384,768]{2,1,0:T(8,128)S(1)} custom-call(bf16[1152,768]{1,0:T(8,128)(2,1)S(1)} %get-tuple-element.119.refs_0_.refs_5_, bf16[1216,768]{1,0:T(8,128)(2,1)S(1)} %get-tuple-element.97.refs_1_.refs_5_), custom_call_target="tpu_custom_call" | custom-call | tf_op jit(solution)/shard_map/weight_term/pallas_call | solution.py:133
  61.9 7.8 %pass_down.2.refs_1_.refs_5_ = bf16[1088,768]{1,0:T(8,128)(2,1)S(1)} custom-call(s32[2]{0:T(128)S(1)} %get-tuple-element.70.refs_0_, bf16[3,192,768]{2,1,0:T(8,128)(2,1)S(1)} %join_rows.6.refs_1_, bf16[3,192,768]{2,1,0:T(8,128)(2,1)S(1)} %collective-permute-done.7.refs_2_, bf16[3,192,768]{2,1,0:T(8,128)(2,1)S(1)} %collective-permute-done.12.refs_3_, ...), custom_call_target="tpu_custom_call" | custom-call | tf_op jit(solution)/shard_map/pass_down/pallas_call | solution.py:133
  69.6 2.0 %weight_term.6 = (bf16[384,768]{1,0:T(8,128)(2,1)S(1)}, bf16[384,768]{1,0:T(8,128)(2,1)S(1)}, bf16[384,768]{1,0:T(8,128)(2,1)S(1)}) custom-call(bf16[1216,768]{1,0:T(8,128)(2,1)S(1)} %get-tuple-element.84.refs_5_.refs_0_, bf16[1088,768]{1,0:T(8,128)(2,1)S(1)} %pass_down.2.refs_1_.refs_5_), custom_call_target="tpu_custom_call" | custom-call | tf_op jit(solution)/shard_map/weight_term/pallas_call | solution.py:133
  72.4 2.0 %weight_term.7 = f32[3,384,768]{2,1,0:T(8,128)S(1)} custom-call(bf16[1216,768]{1,0:T(8,128)(2,1)S(1)} %get-tuple-element.84.refs_5_.refs_0_, bf16[1088,768]{1,0:T(8,128)(2,1)S(1)} %pass_down.2.refs_1_.refs_5_), custom_call_target="tpu_custom_call" | custom-call | tf_op jit(solution)/shard_map/weight_term/pallas_call | solution.py:133
  78.3 8.6 %pass_down.3 = bf16[1024,768]{1,0:T(8,128)(2,1)S(1)} custom-call(s32[2]{0:T(128)S(1)} %iota_multiply_fusion.refs_0_, bf16[3,192,768]{2,1,0:T(8,128)(2,1)S(1)} %join_rows.7.refs_1_, bf16[3,192,768]{2,1,0:T(8,128)(2,1)S(1)} %collective-permute-done.9.refs_2_, bf16[3,192,768]{2,1,0:T(8,128)(2,1)S(1)} %collective-permute-done.10.refs_3_, ...), custom_call_target="tpu_custom_call" | custom-call | tf_op jit(solution)/shard_map/pass_down/pallas_call | solution.py:133
  86.9 1.7 %collective-permute-done.22 = bf16[3,96,768]{2,1,0:T(8,128)(2,1)S(1)} collective-permute-done((bf16[3,96,768]{2,1,0:T(8,128)(2,1)S(1)}, bf16[3,96,768]{2,1,0:T(8,128)(2,1)S(1)}, u32[]{:S(2)}, u32[]{:S(2)}) %collective-permute-start.22) | collective-permute-done | bytes 442400 | tf_op jit(solution)/shard_map/ppermute | solution.py:115
  88.7 1.7 %collective-permute-start.24 = (bf16[3,48,768]{2,1,0:T(8,128)(2,1)S(1)}, bf16[3,48,768]{2,1,0:T(8,128)(2,1)S(1)}, u32[]{:S(2)}, u32[]{:S(2)}) collective-permute-start(bf16[3,48,768]{2,1,0:T(8,128)(2,1)S(1)} %get-tuple-element.116), channel_id=1, source_target_pairs={{0,2},{1,5},{2,0},{3,7},{4,6},{5,1},{6,4},{7,3},{8,10},{9,13},{10,... | collective-permute-start | bytes 663560 | tf_op jit(solution)/shard_map/ppermute | solution.py:115
  91.1 5.1 %layer.3 = bf16[1024,768]{1,0:T(8,128)(2,1)S(1)} custom-call(s32[2]{0:T(128)S(1)} %iota_multiply_fusion.refs_0_, bf16[3,192,768]{2,1,0:T(8,128)(2,1)S(1)} %join_rows.6.refs_1_, bf16[3,192,768]{2,1,0:T(8,128)(2,1)S(1)} %collective-permute-done.7.refs_2_, bf16[3,192,768]{2,1,0:T(8,128)(2,1)S(1)} %collective-permute-done.12.refs_3_, ...), custom_call_target="tpu_custom_call" | custom-call | tf_op jit(solution)/shard_map/layer/pallas_call | solution.py:133
  96.2 3.2 %collective-permute-done.23 = bf16[3,96,768]{2,1,0:T(8,128)(2,1)S(1)} collective-permute-done((bf16[3,96,768]{2,1,0:T(8,128)(2,1)S(1)}, bf16[3,96,768]{2,1,0:T(8,128)(2,1)S(1)}, u32[]{:S(2)}, u32[]{:S(2)}) %collective-permute-start.23) | collective-permute-done | bytes 442400 | tf_op jit(solution)/shard_map/ppermute | solution.py:115
  99.5 1.8 %collective-permute-start.25 = (bf16[3,48,768]{2,1,0:T(8,128)(2,1)S(1)}, bf16[3,48,768]{2,1,0:T(8,128)(2,1)S(1)}, u32[]{:S(2)}, u32[]{:S(2)}) collective-permute-start(bf16[3,48,768]{2,1,0:T(8,128)(2,1)S(1)} %get-tuple-element.127), channel_id=1, source_target_pairs={{0,8},{1,9},{2,10},{3,11},{4,12},{5,13},{6,14},{7,15},{8,0},{9,1},... | collective-permute-start | bytes 663560 | tf_op jit(solution)/shard_map/ppermute | solution.py:115
  102.5 2.6 %collective-permute-start.27 = (bf16[3,24,768]{2,1,0:T(8,128)(2,1)S(1)}, bf16[3,24,768]{2,1,0:T(8,128)(2,1)S(1)}, u32[]{:S(2)}, u32[]{:S(2)}) collective-permute-start(bf16[3,24,768]{2,1,0:T(8,128)(2,1)S(1)} %get-tuple-element.124), channel_id=1, source_target_pairs={{0,16},{1,17},{2,18},{3,19},{4,20},{5,21},{6,22},{7,23},{8,24},{9,... | collective-permute-start | bytes 331784 | tf_op jit(solution)/shard_map/ppermute | solution.py:115
  106.8 3.2 %collective-permute-start.26 = (bf16[3,24,768]{2,1,0:T(8,128)(2,1)S(1)}, bf16[3,24,768]{2,1,0:T(8,128)(2,1)S(1)}, u32[]{:S(2)}, u32[]{:S(2)}) collective-permute-start(bf16[3,24,768]{2,1,0:T(8,128)(2,1)S(1)} %get-tuple-element.130), channel_id=1, source_target_pairs={{0,16},{1,17},{2,18},{3,19},{4,20},{5,21},{6,22},{7,23},{8,24},{9,... | collective-permute-start | bytes 331784 | tf_op jit(solution)/shard_map/ppermute | solution.py:115
  110.6 3.9 %collective-permute-done.26 = bf16[3,24,768]{2,1,0:T(8,128)(2,1)S(1)} collective-permute-done((bf16[3,24,768]{2,1,0:T(8,128)(2,1)S(1)}, bf16[3,24,768]{2,1,0:T(8,128)(2,1)S(1)}, u32[]{:S(2)}, u32[]{:S(2)}) %collective-permute-start.26) | collective-permute-done | bytes 110624 | tf_op jit(solution)/shard_map/ppermute | solution.py:115
  (76 shorter events, 24.2 us)
Async XLA Ops:
  0.6 9.7 %collective-permute-start = (bf16[3,24,768]{2,1,0:T(8,128)(2,1)}, bf16[3,24,768]{2,1,0:T(8,128)(2,1)S(1)}, u32[]{:S(2)}, u32[]{:S(2)}) collective-permute-start(bf16[3,24,768]{2,1,0:T(8,128)(2,1)} %bitcast.23), channel_id=1, source_target_pairs={{0,16},{1,17},{2,18},{3,19},{4,20},{5,21},{6,22},{7,23},{8,24},{9,... | collective-permute-start | bytes 331784 | tf_op jit(solution)/shard_map/ppermute | solution.py:69
  10.4 7.7 %collective-permute-start.2 = (bf16[3,48,768]{2,1,0:T(8,128)(2,1)S(1)}, bf16[3,48,768]{2,1,0:T(8,128)(2,1)S(1)}, u32[]{:S(2)}, u32[]{:S(2)}) collective-permute-start(bf16[3,48,768]{2,1,0:T(8,128)(2,1)S(1)} %pad_maximum_fusion.4.first_ref), channel_id=1, source_target_pairs={{0,8},{1,9},{2,10},{3,11},{4,12},{5,13},{6,14},{7,15},{8,0},{9,1},... | collective-permute-start | bytes 663560 | tf_op jit(solution)/shard_map/ppermute | solution.py:69
  11.3 13.5 %collective-permute-start.4 = (bf16[192,768]{1,0:T(8,128)(2,1)S(1)}, bf16[192,768]{1,0:T(8,128)(2,1)S(1)}, u32[]{:S(2)}, u32[]{:S(2)}) collective-permute-start(bf16[192,768]{1,0:T(8,128)(2,1)S(1)} %get-tuple-element.77), channel_id=1, source_target_pairs={{1,2},{3,4},{5,6},{7,8},{9,10},{11,12},{13,14},{15,16},{17,18},{19... | collective-permute-start | bytes 884744 | tf_op jit(solution)/shard_map/ppermute | solution.py:438
  12.0 12.8 %collective-permute-start.3 = (bf16[192,768]{1,0:T(8,128)(2,1)S(1)}, bf16[192,768]{1,0:T(8,128)(2,1)S(1)}, u32[]{:S(2)}, u32[]{:S(2)}) collective-permute-start(bf16[192,768]{1,0:T(8,128)(2,1)S(1)} %get-tuple-element.76), channel_id=1, source_target_pairs={{0,1},{1,0},{2,3},{3,2},{4,5},{5,4},{6,7},{7,6},{8,9},{9,8},{10,11... | collective-permute-start | bytes 884744 | tf_op jit(solution)/shard_map/ppermute | solution.py:437
  14.9 9.9 %collective-permute-start.1 = (bf16[3,24,768]{2,1,0:T(8,128)(2,1)S(1)}, bf16[3,24,768]{2,1,0:T(8,128)(2,1)S(1)}, u32[]{:S(2)}, u32[]{:S(2)}) collective-permute-start(bf16[3,24,768]{2,1,0:T(8,128)(2,1)S(1)} %bitcast.25), channel_id=1, source_target_pairs={{0,16},{1,17},{2,18},{3,19},{4,20},{5,21},{6,22},{7,23},{8,24},{9,... | collective-permute-start | bytes 331784 | tf_op jit(solution)/shard_map/ppermute | solution.py:69
  18.2 12.6 %collective-permute-start.8 = (bf16[3,96,768]{2,1,0:T(8,128)(2,1)S(1)}, bf16[3,96,768]{2,1,0:T(8,128)(2,1)S(1)}, u32[]{:S(2)}, u32[]{:S(2)}) collective-permute-start(bf16[3,96,768]{2,1,0:T(8,128)(2,1)S(1)} %join_rows.4.first_ref), channel_id=1, source_target_pairs={{0,2},{1,5},{2,0},{3,7},{4,6},{5,1},{6,4},{7,3},{8,10},{9,13},{10,... | collective-permute-start | bytes 1327112 | tf_op jit(solution)/shard_map/ppermute | solution.py:69
  24.8 6.0 %collective-permute-start.5 = (bf16[3,48,768]{2,1,0:T(8,128)(2,1)S(1)}, bf16[3,48,768]{2,1,0:T(8,128)(2,1)S(1)}, u32[]{:S(2)}, u32[]{:S(2)}) collective-permute-start(bf16[3,48,768]{2,1,0:T(8,128)(2,1)S(1)} %pad_maximum_fusion.5.first_ref), channel_id=1, source_target_pairs={{0,2},{1,5},{2,0},{3,7},{4,6},{5,1},{6,4},{7,3},{8,10},{9,13},{10,... | collective-permute-start | bytes 663560 | tf_op jit(solution)/shard_map/ppermute | solution.py:69
  30.9 13.1 %collective-permute-start.9 = (bf16[3,192,768]{2,1,0:T(8,128)(2,1)S(1)}, bf16[3,192,768]{2,1,0:T(8,128)(2,1)S(1)}, u32[]{:S(2)}, u32[]{:S(2)}) collective-permute-start(bf16[3,192,768]{2,1,0:T(8,128)(2,1)S(1)} %join_rows.7.refs_1_), channel_id=1, source_target_pairs={{0,4},{1,3},{2,6},{3,1},{4,0},{5,7},{6,2},{7,5},{8,12},{9,11},{10,... | collective-permute-start | bytes 2654216 | tf_op jit(solution)/shard_map/ppermute | solution.py:69
  31.5 11.0 %collective-permute-start.6 = (bf16[3,96,768]{2,1,0:T(8,128)(2,1)S(1)}, bf16[3,96,768]{2,1,0:T(8,128)(2,1)S(1)}, u32[]{:S(2)}, u32[]{:S(2)}) collective-permute-start(bf16[3,96,768]{2,1,0:T(8,128)(2,1)S(1)} %join_rows.5.first_ref), channel_id=1, source_target_pairs={{0,8},{1,9},{2,10},{3,11},{4,12},{5,13},{6,14},{7,15},{8,0},{9,1},... | collective-permute-start | bytes 1327112 | tf_op jit(solution)/shard_map/ppermute | solution.py:69
  38.5 6.0 %collective-permute-start.10 = (bf16[3,192,768]{2,1,0:T(8,128)(2,1)S(1)}, bf16[3,192,768]{2,1,0:T(8,128)(2,1)S(1)}, u32[]{:S(2)}, u32[]{:S(2)}) collective-permute-start(bf16[3,192,768]{2,1,0:T(8,128)(2,1)S(1)} %join_rows.7.refs_1_), channel_id=1, source_target_pairs={{0,1},{1,0},{2,3},{3,2},{4,5},{5,4},{6,7},{7,6},{8,9},{9,8},{10,11... | collective-permute-start | bytes 2654216 | tf_op jit(solution)/shard_map/ppermute | solution.py:71
  44.0 13.0 %collective-permute-start.7 = (bf16[3,192,768]{2,1,0:T(8,128)(2,1)S(1)}, bf16[3,192,768]{2,1,0:T(8,128)(2,1)S(1)}, u32[]{:S(2)}, u32[]{:S(2)}) collective-permute-start(bf16[3,192,768]{2,1,0:T(8,128)(2,1)S(1)} %join_rows.6.refs_1_), channel_id=1, source_target_pairs={{0,4},{1,3},{2,6},{3,1},{4,0},{5,7},{6,2},{7,5},{8,12},{9,11},{10,... | collective-permute-start | bytes 2654216 | tf_op jit(solution)/shard_map/ppermute | solution.py:69
  55.6 3.5 %collective-permute-start.14 = (bf16[384,768]{1,0:T(8,128)(2,1)S(1)}, bf16[384,768]{1,0:T(8,128)(2,1)S(1)}, u32[]{:S(2)}, u32[]{:S(2)}) collective-permute-start(bf16[384,768]{1,0:T(8,128)(2,1)S(1)} %get-tuple-element.88), channel_id=1, source_target_pairs={{0,1},{1,0},{2,3},{3,2},{4,5},{5,4},{6,7},{7,6},{8,9},{9,8},{10,11... | collective-permute-start | bytes 1769480 | tf_op jit(solution)/shard_map/ppermute | solution.py:91
  55.8 3.3 %collective-permute-start.15 = (bf16[384,768]{1,0:T(8,128)(2,1)S(1)}, bf16[384,768]{1,0:T(8,128)(2,1)S(1)}, u32[]{:S(2)}, u32[]{:S(2)}) collective-permute-start(bf16[384,768]{1,0:T(8,128)(2,1)S(1)} %get-tuple-element.89), channel_id=1, source_target_pairs={{0,1},{1,0},{2,3},{3,2},{4,5},{5,4},{6,7},{7,6},{8,9},{9,8},{10,11... | collective-permute-start | bytes 1769480 | tf_op jit(solution)/shard_map/ppermute | solution.py:91
  56.1 3.2 %collective-permute-start.16 = (bf16[384,768]{1,0:T(8,128)(2,1)S(1)}, bf16[384,768]{1,0:T(8,128)(2,1)S(1)}, u32[]{:S(2)}, u32[]{:S(2)}) collective-permute-start(bf16[384,768]{1,0:T(8,128)(2,1)S(1)} %get-tuple-element.90), channel_id=1, source_target_pairs={{0,1},{1,0},{2,3},{3,2},{4,5},{5,4},{6,7},{7,6},{8,9},{9,8},{10,11... | collective-permute-start | bytes 1769480 | tf_op jit(solution)/shard_map/ppermute | solution.py:91
  56.3 4.4 %collective-permute-start.12 = (bf16[3,192,768]{2,1,0:T(8,128)(2,1)S(1)}, bf16[3,192,768]{2,1,0:T(8,128)(2,1)S(1)}, u32[]{:S(2)}, u32[]{:S(2)}) collective-permute-start(bf16[3,192,768]{2,1,0:T(8,128)(2,1)S(1)} %join_rows.6.refs_1_), channel_id=1, source_target_pairs={{0,1},{1,0},{2,3},{3,2},{4,5},{5,4},{6,7},{7,6},{8,9},{9,8},{10,11... | collective-permute-start | bytes 2654216 | tf_op jit(solution)/shard_map/ppermute | solution.py:71
  57.0 4.8 %collective-permute-start.13 = (bf16[3,192,768]{2,1,0:T(8,128)(2,1)S(1)}, bf16[3,192,768]{2,1,0:T(8,128)(2,1)S(1)}, u32[]{:S(2)}, u32[]{:S(2)}) collective-permute-start(bf16[3,192,768]{2,1,0:T(8,128)(2,1)S(1)} %collective-permute-done.7.refs_2_), channel_id=1, source_target_pairs={{0,1},{1,0},{2,3},{3,2},{4,5},{5,4},{6,7},{7,6},{8,9},{9,8},{10,11... | collective-permute-start | bytes 2654216 | tf_op jit(solution)/shard_map/ppermute | solution.py:71
  60.0 14.5 %collective-permute-start.20 = (bf16[3,192,768]{2,1,0:T(8,128)(2,1)S(1)}, bf16[3,192,768]{2,1,0:T(8,128)(2,1)S(1)}, u32[]{:S(2)}, u32[]{:S(2)}) collective-permute-start(bf16[3,192,768]{2,1,0:T(8,128)(2,1)S(1)} %get-tuple-element.96), channel_id=1, source_target_pairs={{0,4},{1,3},{2,6},{3,1},{4,0},{5,7},{6,2},{7,5},{8,12},{9,11},{10,... | collective-permute-start | bytes 2654216 | tf_op jit(solution)/shard_map/ppermute | solution.py:115
  76.0 14.4 %collective-permute-start.21 = (bf16[3,192,768]{2,1,0:T(8,128)(2,1)S(1)}, bf16[3,192,768]{2,1,0:T(8,128)(2,1)S(1)}, u32[]{:S(2)}, u32[]{:S(2)}) collective-permute-start(bf16[3,192,768]{2,1,0:T(8,128)(2,1)S(1)} %get-tuple-element.110), channel_id=1, source_target_pairs={{0,4},{1,3},{2,6},{3,1},{4,0},{5,7},{6,2},{7,5},{8,12},{9,11},{10,... | collective-permute-start | bytes 2654216 | tf_op jit(solution)/shard_map/ppermute | solution.py:115
  76.7 11.9 %collective-permute-start.22 = (bf16[3,96,768]{2,1,0:T(8,128)(2,1)S(1)}, bf16[3,96,768]{2,1,0:T(8,128)(2,1)S(1)}, u32[]{:S(2)}, u32[]{:S(2)}) collective-permute-start(bf16[3,96,768]{2,1,0:T(8,128)(2,1)S(1)} %get-tuple-element.112), channel_id=1, source_target_pairs={{0,8},{1,9},{2,10},{3,11},{4,12},{5,13},{6,14},{7,15},{8,0},{9,1},... | collective-permute-start | bytes 1327112 | tf_op jit(solution)/shard_map/ppermute | solution.py:115
  88.7 7.5 %collective-permute-start.24 = (bf16[3,48,768]{2,1,0:T(8,128)(2,1)S(1)}, bf16[3,48,768]{2,1,0:T(8,128)(2,1)S(1)}, u32[]{:S(2)}, u32[]{:S(2)}) collective-permute-start(bf16[3,48,768]{2,1,0:T(8,128)(2,1)S(1)} %get-tuple-element.116), channel_id=1, source_target_pairs={{0,2},{1,5},{2,0},{3,7},{4,6},{5,1},{6,4},{7,3},{8,10},{9,13},{10,... | collective-permute-start | bytes 663560 | tf_op jit(solution)/shard_map/ppermute | solution.py:115
  90.6 8.8 %collective-permute-start.23 = (bf16[3,96,768]{2,1,0:T(8,128)(2,1)S(1)}, bf16[3,96,768]{2,1,0:T(8,128)(2,1)S(1)}, u32[]{:S(2)}, u32[]{:S(2)}) collective-permute-start(bf16[3,96,768]{2,1,0:T(8,128)(2,1)S(1)} %get-tuple-element.118), channel_id=1, source_target_pairs={{0,2},{1,5},{2,0},{3,7},{4,6},{5,1},{6,4},{7,3},{8,10},{9,13},{10,... | collective-permute-start | bytes 1327112 | tf_op jit(solution)/shard_map/ppermute | solution.py:115
  99.5 7.2 %collective-permute-start.25 = (bf16[3,48,768]{2,1,0:T(8,128)(2,1)S(1)}, bf16[3,48,768]{2,1,0:T(8,128)(2,1)S(1)}, u32[]{:S(2)}, u32[]{:S(2)}) collective-permute-start(bf16[3,48,768]{2,1,0:T(8,128)(2,1)S(1)} %get-tuple-element.127), channel_id=1, source_target_pairs={{0,8},{1,9},{2,10},{3,11},{4,12},{5,13},{6,14},{7,15},{8,0},{9,1},... | collective-permute-start | bytes 663560 | tf_op jit(solution)/shard_map/ppermute | solution.py:115
  102.5 7.4 %collective-permute-start.27 = (bf16[3,24,768]{2,1,0:T(8,128)(2,1)S(1)}, bf16[3,24,768]{2,1,0:T(8,128)(2,1)S(1)}, u32[]{:S(2)}, u32[]{:S(2)}) collective-permute-start(bf16[3,24,768]{2,1,0:T(8,128)(2,1)S(1)} %get-tuple-element.124), channel_id=1, source_target_pairs={{0,16},{1,17},{2,18},{3,19},{4,20},{5,21},{6,22},{7,23},{8,24},{9,... | collective-permute-start | bytes 331784 | tf_op jit(solution)/shard_map/ppermute | solution.py:115
  106.8 7.8 %collective-permute-start.26 = (bf16[3,24,768]{2,1,0:T(8,128)(2,1)S(1)}, bf16[3,24,768]{2,1,0:T(8,128)(2,1)S(1)}, u32[]{:S(2)}, u32[]{:S(2)}) collective-permute-start(bf16[3,24,768]{2,1,0:T(8,128)(2,1)S(1)} %get-tuple-element.130), channel_id=1, source_target_pairs={{0,16},{1,17},{2,18},{3,19},{4,20},{5,21},{6,22},{7,23},{8,24},{9,... | collective-permute-start | bytes 331784 | tf_op jit(solution)/shard_map/ppermute | solution.py:115
  (8 other events, 56.0 us)

commit v2 on v1

--- a/solution.py
+++ b/solution.py
@@ -143,18 +143,18 @@
     )(*scalars, *on_chip(*arrays))
 
 
-def over_blocks(length, body, unrolled):
-    rows = length // BLOCKS
+def over_blocks(length, body, unrolled, blocks=BLOCKS):
+    rows = length // blocks
 
     def step(index, carry):
         body(index * rows, rows)
         return carry
 
     if unrolled:
-        for index in range(BLOCKS):
+        for index in range(blocks):
             body(index * rows, rows)
     else:
-        lax.fori_loop(0, BLOCKS, step, 0)
+        lax.fori_loop(0, blocks, step, 0)
 
 
 def span(first, rows):
@@ -269,7 +269,7 @@
             ).astype(jnp.bfloat16)
             activate(first, rel_ref.at[span(first, rows)], next_ref)
 
-    over_blocks(length, block, follow)
+    over_blocks(length, block, follow, 6 if follow else BLOCKS)
 
 
 def layer(edges, pieces, active, layer_in, offset, length, spacing, turn=None):
@@ -495,8 +495,8 @@
         turn_one,
         DILATION_A,
     )
-    sent = scatter_two.add(input_grad)
-    sent = scatter_one.add(sent)
+    sent = scatter_one.add(input_grad)
+    sent = scatter_two.add(sent)
     (outputs,) = layer(
         own_edges,
         full_two,

time: 115 us -> 116 us (level)
  starting transfers between devices: 31.2 us -> 32.6 us
    ppermute x8, starting transfers between devices: 12.6 us -> 14 us  [go(): self.arrived = lax.ppermute(send, 'seq', pairs)]
  transfers between devices with their start and end apart: 28 -> 28, of which waited for: 14 -> 15; matrix products, arithmetic and copies ran while one was open for 6% -> 5% of each run, Pallas kernels for 37% -> 36%
where the time goes in v2:
time: 116 us
  Pallas kernels  42.4 us (37%)
  starting transfers between devices  32.6 us (28%)
  waiting for transfers between devices  32.5 us (28%)
  other arithmetic  4.41 us (4%)
  local copies, waits for them, and re-layouts  3.47 us (3%)
    pallas_call x13, Pallas kernels, call(): pl.pallas_call(kernel, in_specs=[pl.BlockSpec(memory_space=pltpu.SMEM)] *...  42.4 us
    ppermute x8, waiting for transfers between devices, send(): lax.ppermute(self.held, 'seq', step_pairs(count, self.route, self.step))  19.5 us
    ppermute x8, starting transfers between devices, go(): self.arrived = lax.ppermute(send, 'seq', pairs)  14 us
    ppermute x8, starting transfers between devices, send(): lax.ppermute(self.held, 'seq', step_pairs(count, self.route, self.step))  13.1 us
    ppermute x8, waiting for transfers between devices, go(): self.arrived = lax.ppermute(send, 'seq', pairs)  9.06 us
    ppermute x4, waiting for transfers between devices, send(): lax.ppermute(self.held, 'seq', core_pairs(count))  3.06 us
    ppermute x1, starting transfers between devices, per_device(): inner = lax.ppermute(after(inner, joined), 'seq', core_pairs(count))  2.9 us
  transfers between devices with their start and end apart: 28, of which 15 were waited for; matrix products, arithmetic and copies ran while one was open for 5% of the time, Pallas kernels for 36%

profile of v2, /device:TPU:0, one launch (start us, length us, event | category | flops | bytes accessed | tf_op | source)
XLA Modules:
  0.0 116.3 jit_solution(13303907863896964107)
XLA Ops:
  0.6 4.1 %collective-permute-start = (bf16[3,24,768]{2,1,0:T(8,128)(2,1)}, bf16[3,24,768]{2,1,0:T(8,128)(2,1)S(1)}, u32[]{:S(2)}, u32[]{:S(2)}) collective-permute-start(bf16[3,24,768]{2,1,0:T(8,128)(2,1)} %bitcast.23), channel_id=1, source_target_pairs={{0,16},{1,17},{2,18},{3,19},{4,20},{5,21},{6,22},{7,23},{8,24},{9,... | collective-permute-start | bytes 331784 | tf_op jit(solution)/shard_map/ppermute | solution.py:69
  7.0 3.4 %collective-permute-done = bf16[3,24,768]{2,1,0:T(8,128)(2,1)S(1)} collective-permute-done((bf16[3,24,768]{2,1,0:T(8,128)(2,1)}, bf16[3,24,768]{2,1,0:T(8,128)(2,1)S(1)}, u32[]{:S(2)}, u32[]{:S(2)}) %collective-permute-start) | collective-permute-done | bytes 110624 | tf_op jit(solution)/shard_map/ppermute | solution.py:69
  12.0 2.9 %collective-permute-start.3 = (bf16[192,768]{1,0:T(8,128)(2,1)S(1)}, bf16[192,768]{1,0:T(8,128)(2,1)S(1)}, u32[]{:S(2)}, u32[]{:S(2)}) collective-permute-start(bf16[192,768]{1,0:T(8,128)(2,1)S(1)} %get-tuple-element.76), channel_id=1, source_target_pairs={{0,1},{1,0},{2,3},{3,2},{4,5},{5,4},{6,7},{7,6},{8,9},{9,8},{10,11... | collective-permute-start | bytes 884744 | tf_op jit(solution)/shard_map/ppermute | solution.py:437
  14.9 3.3 %collective-permute-start.1 = (bf16[3,24,768]{2,1,0:T(8,128)(2,1)S(1)}, bf16[3,24,768]{2,1,0:T(8,128)(2,1)S(1)}, u32[]{:S(2)}, u32[]{:S(2)}) collective-permute-start(bf16[3,24,768]{2,1,0:T(8,128)(2,1)S(1)} %bitcast.25), channel_id=1, source_target_pairs={{0,16},{1,17},{2,18},{3,19},{4,20},{5,21},{6,22},{7,23},{8,24},{9,... | collective-permute-start | bytes 331784 | tf_op jit(solution)/shard_map/ppermute | solution.py:69
  19.7 5.0 %collective-permute-done.1 = bf16[3,24,768]{2,1,0:T(8,128)(2,1)S(1)} collective-permute-done((bf16[3,24,768]{2,1,0:T(8,128)(2,1)S(1)}, bf16[3,24,768]{2,1,0:T(8,128)(2,1)S(1)}, u32[]{:S(2)}, u32[]{:S(2)}) %collective-permute-start.1) | collective-permute-done | bytes 110624 | tf_op jit(solution)/shard_map/ppermute | solution.py:69
  25.4 5.4 %collective-permute-done.5.second_ref = bf16[3,48,768]{2,1,0:T(8,128)(2,1)S(1)} collective-permute-done((bf16[3,48,768]{2,1,0:T(8,128)(2,1)S(1)}, bf16[3,48,768]{2,1,0:T(8,128)(2,1)S(1)}, u32[]{:S(2)}, u32[]{:S(2)}) %collective-permute-start.5) | collective-permute-done | bytes 221216 | tf_op jit(solution)/shard_map/ppermute | solution.py:69
  33.0 5.5 %first_active.1 = (bf16[1216,768]{1,0:T(8,128)(2,1)S(1)}, bf16[1216,768]{1,0:T(8,128)(2,1)S(1)}, bf16[1216,768]{1,0:T(8,128)(2,1)S(1)}, bf16[1216,768]{1,0:T(8,128)(2,1)S(1)}, bf16[1088,768]{1,0:T(8,128)(2,1)S(1)}) custom-call(s32[1]{0:T(128)} %bitcast.4.refs_0_, bf16[1024,768]{1,0:T(8,128)(2,1)S(1)} %copy-done, bf16[1024,768]{1,0:T(8,128)(2,1)S(1)} %copy-done.1, ...), custom_call_target="tpu_custom_call" | custom-call | tf_op jit(solution)/shard_map/first_active/pallas_call | solution.py:133
  38.6 4.0 %collective-permute-done.6.second_ref = bf16[3,96,768]{2,1,0:T(8,128)(2,1)S(1)} collective-permute-done((bf16[3,96,768]{2,1,0:T(8,128)(2,1)S(1)}, bf16[3,96,768]{2,1,0:T(8,128)(2,1)S(1)}, u32[]{:S(2)}, u32[]{:S(2)}) %collective-permute-start.6) | collective-permute-done | bytes 442400 | tf_op jit(solution)/shard_map/ppermute | solution.py:69
  44.6 1.8 %collective-permute-done.11.refs_4_ = bf16[3,192,768]{2,1,0:T(8,128)(2,1)S(1)} collective-permute-done((bf16[3,192,768]{2,1,0:T(8,128)(2,1)S(1)}, bf16[3,192,768]{2,1,0:T(8,128)(2,1)S(1)}, u32[]{:S(2)}, u32[]{:S(2)}) %collective-permute-start.11) | collective-permute-done | bytes 884768 | tf_op jit(solution)/shard_map/ppermute | solution.py:71
  46.4 7.0 %layer.2 = (bf16[1152,768]{1,0:T(8,128)(2,1)S(1)}, bf16[1152,768]{1,0:T(8,128)(2,1)S(1)}, bf16[1152,768]{1,0:T(8,128)(2,1)S(1)}) custom-call(s32[2]{0:T(128)S(1)} %get-tuple-element.69.refs_0_, bf16[3,192,768]{2,1,0:T(8,128)(2,1)S(1)} %join_rows.7.refs_1_, bf16[3,192,768]{2,1,0:T(8,128)(2,1)S(1)} %collective-permute-done.9.refs_2_, ...), custom_call_target="tpu_custom_call" | custom-call | tf_op jit(solution)/shard_map/layer/pallas_call | solution.py:133
  53.4 2.0 %weight_term.4 = (bf16[384,768]{1,0:T(8,128)(2,1)S(1)}, bf16[384,768]{1,0:T(8,128)(2,1)S(1)}, bf16[384,768]{1,0:T(8,128)(2,1)S(1)}) custom-call(bf16[1152,768]{1,0:T(8,128)(2,1)S(1)} %get-tuple-element.119.refs_0_.refs_5_, bf16[1216,768]{1,0:T(8,128)(2,1)S(1)} %get-tuple-element.98.refs_1_.refs_5_), custom_call_target="tpu_custom_call" | custom-call | tf_op jit(solution)/shard_map/weight_term/pallas_call | solution.py:133
  57.0 2.0 %weight_term.5 = f32[3,384,768]{2,1,0:T(8,128)S(1)} custom-call(bf16[1152,768]{1,0:T(8,128)(2,1)S(1)} %get-tuple-element.119.refs_0_.refs_5_, bf16[1216,768]{1,0:T(8,128)(2,1)S(1)} %get-tuple-element.98.refs_1_.refs_5_), custom_call_target="tpu_custom_call" | custom-call | tf_op jit(solution)/shard_map/weight_term/pallas_call | solution.py:133
  61.8 7.8 %pass_down.2.refs_1_.refs_5_ = bf16[1088,768]{1,0:T(8,128)(2,1)S(1)} custom-call(s32[2]{0:T(128)S(1)} %get-tuple-element.70.refs_0_, bf16[3,192,768]{2,1,0:T(8,128)(2,1)S(1)} %join_rows.6.refs_1_, bf16[3,192,768]{2,1,0:T(8,128)(2,1)S(1)} %collective-permute-done.7.refs_2_, bf16[3,192,768]{2,1,0:T(8,128)(2,1)S(1)} %collective-permute-done.12.refs_3_, ...), custom_call_target="tpu_custom_call" | custom-call | tf_op jit(solution)/shard_map/pass_down/pallas_call | solution.py:133
  69.6 2.0 %weight_term.6 = (bf16[384,768]{1,0:T(8,128)(2,1)S(1)}, bf16[384,768]{1,0:T(8,128)(2,1)S(1)}, bf16[384,768]{1,0:T(8,128)(2,1)S(1)}) custom-call(bf16[1216,768]{1,0:T(8,128)(2,1)S(1)} %get-tuple-element.84.refs_5_.refs_0_, bf16[1088,768]{1,0:T(8,128)(2,1)S(1)} %pass_down.2.refs_1_.refs_5_), custom_call_target="tpu_custom_call" | custom-call | tf_op jit(solution)/shard_map/weight_term/pallas_call | solution.py:133
  72.3 2.0 %weight_term.7 = f32[3,384,768]{2,1,0:T(8,128)S(1)} custom-call(bf16[1216,768]{1,0:T(8,128)(2,1)S(1)} %get-tuple-element.84.refs_5_.refs_0_, bf16[1088,768]{1,0:T(8,128)(2,1)S(1)} %pass_down.2.refs_1_.refs_5_), custom_call_target="tpu_custom_call" | custom-call | tf_op jit(solution)/shard_map/weight_term/pallas_call | solution.py:133
  76.6 1.6 %collective-permute-start.21 = (bf16[3,96,768]{2,1,0:T(8,128)(2,1)S(1)}, bf16[3,96,768]{2,1,0:T(8,128)(2,1)S(1)}, u32[]{:S(2)}, u32[]{:S(2)}) collective-permute-start(bf16[3,96,768]{2,1,0:T(8,128)(2,1)S(1)} %get-tuple-element.111), channel_id=1, source_target_pairs={{0,8},{1,9},{2,10},{3,11},{4,12},{5,13},{6,14},{7,15},{8,0},{9,1},... | collective-permute-start | bytes 1327112 | tf_op jit(solution)/shard_map/ppermute | solution.py:115
  78.2 8.6 %pass_down.3 = bf16[1024,768]{1,0:T(8,128)(2,1)S(1)} custom-call(s32[2]{0:T(128)S(1)} %iota_multiply_fusion.refs_0_, bf16[3,192,768]{2,1,0:T(8,128)(2,1)S(1)} %join_rows.7.refs_1_, bf16[3,192,768]{2,1,0:T(8,128)(2,1)S(1)} %collective-permute-done.9.refs_2_, bf16[3,192,768]{2,1,0:T(8,128)(2,1)S(1)} %collective-permute-done.10.refs_3_, ...), custom_call_target="tpu_custom_call" | custom-call | tf_op jit(solution)/shard_map/pass_down/pallas_call | solution.py:133
  86.9 2.2 %collective-permute-done.22 = bf16[3,192,768]{2,1,0:T(8,128)(2,1)S(1)} collective-permute-done((bf16[3,192,768]{2,1,0:T(8,128)(2,1)S(1)}, bf16[3,192,768]{2,1,0:T(8,128)(2,1)S(1)}, u32[]{:S(2)}, u32[]{:S(2)}) %collective-permute-start.22) | collective-permute-done | bytes 884768 | tf_op jit(solution)/shard_map/ppermute | solution.py:115
  91.4 5.1 %layer.3 = bf16[1024,768]{1,0:T(8,128)(2,1)S(1)} custom-call(s32[2]{0:T(128)S(1)} %iota_multiply_fusion.refs_0_, bf16[3,192,768]{2,1,0:T(8,128)(2,1)S(1)} %join_rows.6.refs_1_, bf16[3,192,768]{2,1,0:T(8,128)(2,1)S(1)} %collective-permute-done.7.refs_2_, bf16[3,192,768]{2,1,0:T(8,128)(2,1)S(1)} %collective-permute-done.12.refs_3_, ...), custom_call_target="tpu_custom_call" | custom-call | tf_op jit(solution)/shard_map/layer/pallas_call | solution.py:133
  96.6 3.5 %collective-permute-done.23 = bf16[3,96,768]{2,1,0:T(8,128)(2,1)S(1)} collective-permute-done((bf16[3,96,768]{2,1,0:T(8,128)(2,1)S(1)}, bf16[3,96,768]{2,1,0:T(8,128)(2,1)S(1)}, u32[]{:S(2)}, u32[]{:S(2)}) %collective-permute-start.23) | collective-permute-done | bytes 442400 | tf_op jit(solution)/shard_map/ppermute | solution.py:115
  100.2 2.0 %collective-permute-start.25 = (bf16[3,48,768]{2,1,0:T(8,128)(2,1)S(1)}, bf16[3,48,768]{2,1,0:T(8,128)(2,1)S(1)}, u32[]{:S(2)}, u32[]{:S(2)}) collective-permute-start(bf16[3,48,768]{2,1,0:T(8,128)(2,1)S(1)} %get-tuple-element.127), channel_id=1, source_target_pairs={{0,8},{1,9},{2,10},{3,11},{4,12},{5,13},{6,14},{7,15},{8,0},{9,1},... | collective-permute-start | bytes 663560 | tf_op jit(solution)/shard_map/ppermute | solution.py:115
  104.5 1.6 %collective-permute-start.27 = (bf16[3,24,768]{2,1,0:T(8,128)(2,1)S(1)}, bf16[3,24,768]{2,1,0:T(8,128)(2,1)S(1)}, u32[]{:S(2)}, u32[]{:S(2)}) collective-permute-start(bf16[3,24,768]{2,1,0:T(8,128)(2,1)S(1)} %get-tuple-element.124), channel_id=1, source_target_pairs={{0,16},{1,17},{2,18},{3,19},{4,20},{5,21},{6,22},{7,23},{8,24},{9,... | collective-permute-start | bytes 331784 | tf_op jit(solution)/shard_map/ppermute | solution.py:115
  106.3 5.4 %collective-permute-start.26 = (bf16[3,24,768]{2,1,0:T(8,128)(2,1)S(1)}, bf16[3,24,768]{2,1,0:T(8,128)(2,1)S(1)}, u32[]{:S(2)}, u32[]{:S(2)}) collective-permute-start(bf16[3,24,768]{2,1,0:T(8,128)(2,1)S(1)} %get-tuple-element.130), channel_id=1, source_target_pairs={{0,16},{1,17},{2,18},{3,19},{4,20},{5,21},{6,22},{7,23},{8,24},{9,... | collective-permute-start | bytes 331784 | tf_op jit(solution)/shard_map/ppermute | solution.py:115
  111.7 2.8 %collective-permute-done.27 = bf16[3,24,768]{2,1,0:T(8,128)(2,1)S(1)} collective-permute-done((bf16[3,24,768]{2,1,0:T(8,128)(2,1)S(1)}, bf16[3,24,768]{2,1,0:T(8,128)(2,1)S(1)}, u32[]{:S(2)}, u32[]{:S(2)}) %collective-permute-start.27) | collective-permute-done | bytes 110624 | tf_op jit(solution)/shard_map/ppermute | solution.py:115
  (76 shorter events, 24.3 us)
Async XLA Ops:
  0.6 9.7 %collective-permute-start = (bf16[3,24,768]{2,1,0:T(8,128)(2,1)}, bf16[3,24,768]{2,1,0:T(8,128)(2,1)S(1)}, u32[]{:S(2)}, u32[]{:S(2)}) collective-permute-start(bf16[3,24,768]{2,1,0:T(8,128)(2,1)} %bitcast.23), channel_id=1, source_target_pairs={{0,16},{1,17},{2,18},{3,19},{4,20},{5,21},{6,22},{7,23},{8,24},{9,... | collective-permute-start | bytes 331784 | tf_op jit(solution)/shard_map/ppermute | solution.py:69
  10.4 7.7 %collective-permute-start.2 = (bf16[3,48,768]{2,1,0:T(8,128)(2,1)S(1)}, bf16[3,48,768]{2,1,0:T(8,128)(2,1)S(1)}, u32[]{:S(2)}, u32[]{:S(2)}) collective-permute-start(bf16[3,48,768]{2,1,0:T(8,128)(2,1)S(1)} %pad_maximum_fusion.4.first_ref), channel_id=1, source_target_pairs={{0,8},{1,9},{2,10},{3,11},{4,12},{5,13},{6,14},{7,15},{8,0},{9,1},... | collective-permute-start | bytes 663560 | tf_op jit(solution)/shard_map/ppermute | solution.py:69
  11.3 13.5 %collective-permute-start.4 = (bf16[192,768]{1,0:T(8,128)(2,1)S(1)}, bf16[192,768]{1,0:T(8,128)(2,1)S(1)}, u32[]{:S(2)}, u32[]{:S(2)}) collective-permute-start(bf16[192,768]{1,0:T(8,128)(2,1)S(1)} %get-tuple-element.77), channel_id=1, source_target_pairs={{1,2},{3,4},{5,6},{7,8},{9,10},{11,12},{13,14},{15,16},{17,18},{19... | collective-permute-start | bytes 884744 | tf_op jit(solution)/shard_map/ppermute | solution.py:438
  12.0 12.8 %collective-permute-start.3 = (bf16[192,768]{1,0:T(8,128)(2,1)S(1)}, bf16[192,768]{1,0:T(8,128)(2,1)S(1)}, u32[]{:S(2)}, u32[]{:S(2)}) collective-permute-start(bf16[192,768]{1,0:T(8,128)(2,1)S(1)} %get-tuple-element.76), channel_id=1, source_target_pairs={{0,1},{1,0},{2,3},{3,2},{4,5},{5,4},{6,7},{7,6},{8,9},{9,8},{10,11... | collective-permute-start | bytes 884744 | tf_op jit(solution)/shard_map/ppermute | solution.py:437
  14.9 9.9 %collective-permute-start.1 = (bf16[3,24,768]{2,1,0:T(8,128)(2,1)S(1)}, bf16[3,24,768]{2,1,0:T(8,128)(2,1)S(1)}, u32[]{:S(2)}, u32[]{:S(2)}) collective-permute-start(bf16[3,24,768]{2,1,0:T(8,128)(2,1)S(1)} %bitcast.25), channel_id=1, source_target_pairs={{0,16},{1,17},{2,18},{3,19},{4,20},{5,21},{6,22},{7,23},{8,24},{9,... | collective-permute-start | bytes 331784 | tf_op jit(solution)/shard_map/ppermute | solution.py:69
  18.2 12.6 %collective-permute-start.8 = (bf16[3,96,768]{2,1,0:T(8,128)(2,1)S(1)}, bf16[3,96,768]{2,1,0:T(8,128)(2,1)S(1)}, u32[]{:S(2)}, u32[]{:S(2)}) collective-permute-start(bf16[3,96,768]{2,1,0:T(8,128)(2,1)S(1)} %join_rows.4.first_ref), channel_id=1, source_target_pairs={{0,2},{1,5},{2,0},{3,7},{4,6},{5,1},{6,4},{7,3},{8,10},{9,13},{10,... | collective-permute-start | bytes 1327112 | tf_op jit(solution)/shard_map/ppermute | solution.py:69
  24.8 6.0 %collective-permute-start.5 = (bf16[3,48,768]{2,1,0:T(8,128)(2,1)S(1)}, bf16[3,48,768]{2,1,0:T(8,128)(2,1)S(1)}, u32[]{:S(2)}, u32[]{:S(2)}) collective-permute-start(bf16[3,48,768]{2,1,0:T(8,128)(2,1)S(1)} %pad_maximum_fusion.5.first_ref), channel_id=1, source_target_pairs={{0,2},{1,5},{2,0},{3,7},{4,6},{5,1},{6,4},{7,3},{8,10},{9,13},{10,... | collective-permute-start | bytes 663560 | tf_op jit(solution)/shard_map/ppermute | solution.py:69
  30.9 13.1 %collective-permute-start.9 = (bf16[3,192,768]{2,1,0:T(8,128)(2,1)S(1)}, bf16[3,192,768]{2,1,0:T(8,128)(2,1)S(1)}, u32[]{:S(2)}, u32[]{:S(2)}) collective-permute-start(bf16[3,192,768]{2,1,0:T(8,128)(2,1)S(1)} %join_rows.7.refs_1_), channel_id=1, source_target_pairs={{0,4},{1,3},{2,6},{3,1},{4,0},{5,7},{6,2},{7,5},{8,12},{9,11},{10,... | collective-permute-start | bytes 2654216 | tf_op jit(solution)/shard_map/ppermute | solution.py:69
  31.5 11.0 %collective-permute-start.6 = (bf16[3,96,768]{2,1,0:T(8,128)(2,1)S(1)}, bf16[3,96,768]{2,1,0:T(8,128)(2,1)S(1)}, u32[]{:S(2)}, u32[]{:S(2)}) collective-permute-start(bf16[3,96,768]{2,1,0:T(8,128)(2,1)S(1)} %join_rows.5.first_ref), channel_id=1, source_target_pairs={{0,8},{1,9},{2,10},{3,11},{4,12},{5,13},{6,14},{7,15},{8,0},{9,1},... | collective-permute-start | bytes 1327112 | tf_op jit(solution)/shard_map/ppermute | solution.py:69
  38.5 6.0 %collective-permute-start.10 = (bf16[3,192,768]{2,1,0:T(8,128)(2,1)S(1)}, bf16[3,192,768]{2,1,0:T(8,128)(2,1)S(1)}, u32[]{:S(2)}, u32[]{:S(2)}) collective-permute-start(bf16[3,192,768]{2,1,0:T(8,128)(2,1)S(1)} %join_rows.7.refs_1_), channel_id=1, source_target_pairs={{0,1},{1,0},{2,3},{3,2},{4,5},{5,4},{6,7},{7,6},{8,9},{9,8},{10,11... | collective-permute-start | bytes 2654216 | tf_op jit(solution)/shard_map/ppermute | solution.py:71
  44.0 13.0 %collective-permute-start.7 = (bf16[3,192,768]{2,1,0:T(8,128)(2,1)S(1)}, bf16[3,192,768]{2,1,0:T(8,128)(2,1)S(1)}, u32[]{:S(2)}, u32[]{:S(2)}) collective-permute-start(bf16[3,192,768]{2,1,0:T(8,128)(2,1)S(1)} %join_rows.6.refs_1_), channel_id=1, source_target_pairs={{0,4},{1,3},{2,6},{3,1},{4,0},{5,7},{6,2},{7,5},{8,12},{9,11},{10,... | collective-permute-start | bytes 2654216 | tf_op jit(solution)/shard_map/ppermute | solution.py:69
  55.5 3.6 %collective-permute-start.14 = (bf16[384,768]{1,0:T(8,128)(2,1)S(1)}, bf16[384,768]{1,0:T(8,128)(2,1)S(1)}, u32[]{:S(2)}, u32[]{:S(2)}) collective-permute-start(bf16[384,768]{1,0:T(8,128)(2,1)S(1)} %get-tuple-element.88), channel_id=1, source_target_pairs={{0,1},{1,0},{2,3},{3,2},{4,5},{5,4},{6,7},{7,6},{8,9},{9,8},{10,11... | collective-permute-start | bytes 1769480 | tf_op jit(solution)/shard_map/ppermute | solution.py:91
  55.7 3.4 %collective-permute-start.15 = (bf16[384,768]{1,0:T(8,128)(2,1)S(1)}, bf16[384,768]{1,0:T(8,128)(2,1)S(1)}, u32[]{:S(2)}, u32[]{:S(2)}) collective-permute-start(bf16[384,768]{1,0:T(8,128)(2,1)S(1)} %get-tuple-element.89), channel_id=1, source_target_pairs={{0,1},{1,0},{2,3},{3,2},{4,5},{5,4},{6,7},{7,6},{8,9},{9,8},{10,11... | collective-permute-start | bytes 1769480 | tf_op jit(solution)/shard_map/ppermute | solution.py:91
  56.1 3.2 %collective-permute-start.16 = (bf16[384,768]{1,0:T(8,128)(2,1)S(1)}, bf16[384,768]{1,0:T(8,128)(2,1)S(1)}, u32[]{:S(2)}, u32[]{:S(2)}) collective-permute-start(bf16[384,768]{1,0:T(8,128)(2,1)S(1)} %get-tuple-element.90), channel_id=1, source_target_pairs={{0,1},{1,0},{2,3},{3,2},{4,5},{5,4},{6,7},{7,6},{8,9},{9,8},{10,11... | collective-permute-start | bytes 1769480 | tf_op jit(solution)/shard_map/ppermute | solution.py:91
  56.2 4.4 %collective-permute-start.12 = (bf16[3,192,768]{2,1,0:T(8,128)(2,1)S(1)}, bf16[3,192,768]{2,1,0:T(8,128)(2,1)S(1)}, u32[]{:S(2)}, u32[]{:S(2)}) collective-permute-start(bf16[3,192,768]{2,1,0:T(8,128)(2,1)S(1)} %join_rows.6.refs_1_), channel_id=1, source_target_pairs={{0,1},{1,0},{2,3},{3,2},{4,5},{5,4},{6,7},{7,6},{8,9},{9,8},{10,11... | collective-permute-start | bytes 2654216 | tf_op jit(solution)/shard_map/ppermute | solution.py:71
  57.0 4.7 %collective-permute-start.13 = (bf16[3,192,768]{2,1,0:T(8,128)(2,1)S(1)}, bf16[3,192,768]{2,1,0:T(8,128)(2,1)S(1)}, u32[]{:S(2)}, u32[]{:S(2)}) collective-permute-start(bf16[3,192,768]{2,1,0:T(8,128)(2,1)S(1)} %collective-permute-done.7.refs_2_), channel_id=1, source_target_pairs={{0,1},{1,0},{2,3},{3,2},{4,5},{5,4},{6,7},{7,6},{8,9},{9,8},{10,11... | collective-permute-start | bytes 2654216 | tf_op jit(solution)/shard_map/ppermute | solution.py:71
  59.9 14.5 %collective-permute-start.17 = (bf16[3,192,768]{2,1,0:T(8,128)(2,1)S(1)}, bf16[3,192,768]{2,1,0:T(8,128)(2,1)S(1)}, u32[]{:S(2)}, u32[]{:S(2)}) collective-permute-start(bf16[3,192,768]{2,1,0:T(8,128)(2,1)S(1)} %get-tuple-element.97), channel_id=1, source_target_pairs={{0,4},{1,3},{2,6},{3,1},{4,0},{5,7},{6,2},{7,5},{8,12},{9,11},{10,... | collective-permute-start | bytes 2654216 | tf_op jit(solution)/shard_map/ppermute | solution.py:115
  76.0 13.1 %collective-permute-start.22 = (bf16[3,192,768]{2,1,0:T(8,128)(2,1)S(1)}, bf16[3,192,768]{2,1,0:T(8,128)(2,1)S(1)}, u32[]{:S(2)}, u32[]{:S(2)}) collective-permute-start(bf16[3,192,768]{2,1,0:T(8,128)(2,1)S(1)} %get-tuple-element.110), channel_id=1, source_target_pairs={{0,4},{1,3},{2,6},{3,1},{4,0},{5,7},{6,2},{7,5},{8,12},{9,11},{10,... | collective-permute-start | bytes 2654216 | tf_op jit(solution)/shard_map/ppermute | solution.py:115
  76.6 12.6 %collective-permute-start.21 = (bf16[3,96,768]{2,1,0:T(8,128)(2,1)S(1)}, bf16[3,96,768]{2,1,0:T(8,128)(2,1)S(1)}, u32[]{:S(2)}, u32[]{:S(2)}) collective-permute-start(bf16[3,96,768]{2,1,0:T(8,128)(2,1)S(1)} %get-tuple-element.111), channel_id=1, source_target_pairs={{0,8},{1,9},{2,10},{3,11},{4,12},{5,13},{6,14},{7,15},{8,0},{9,1},... | collective-permute-start | bytes 1327112 | tf_op jit(solution)/shard_map/ppermute | solution.py:115
  89.4 7.2 %collective-permute-start.24 = (bf16[3,48,768]{2,1,0:T(8,128)(2,1)S(1)}, bf16[3,48,768]{2,1,0:T(8,128)(2,1)S(1)}, u32[]{:S(2)}, u32[]{:S(2)}) collective-permute-start(bf16[3,48,768]{2,1,0:T(8,128)(2,1)S(1)} %get-tuple-element.118), channel_id=1, source_target_pairs={{0,2},{1,5},{2,0},{3,7},{4,6},{5,1},{6,4},{7,3},{8,10},{9,13},{10,... | collective-permute-start | bytes 663560 | tf_op jit(solution)/shard_map/ppermute | solution.py:115
  90.4 9.7 %collective-permute-start.23 = (bf16[3,96,768]{2,1,0:T(8,128)(2,1)S(1)}, bf16[3,96,768]{2,1,0:T(8,128)(2,1)S(1)}, u32[]{:S(2)}, u32[]{:S(2)}) collective-permute-start(bf16[3,96,768]{2,1,0:T(8,128)(2,1)S(1)} %get-tuple-element.116), channel_id=1, source_target_pairs={{0,2},{1,5},{2,0},{3,7},{4,6},{5,1},{6,4},{7,3},{8,10},{9,13},{10,... | collective-permute-start | bytes 1327112 | tf_op jit(solution)/shard_map/ppermute | solution.py:115
  100.2 6.1 %collective-permute-start.25 = (bf16[3,48,768]{2,1,0:T(8,128)(2,1)S(1)}, bf16[3,48,768]{2,1,0:T(8,128)(2,1)S(1)}, u32[]{:S(2)}, u32[]{:S(2)}) collective-permute-start(bf16[3,48,768]{2,1,0:T(8,128)(2,1)S(1)} %get-tuple-element.127), channel_id=1, source_target_pairs={{0,8},{1,9},{2,10},{3,11},{4,12},{5,13},{6,14},{7,15},{8,0},{9,1},... | collective-permute-start | bytes 663560 | tf_op jit(solution)/shard_map/ppermute | solution.py:115
  104.5 9.9 %collective-permute-start.27 = (bf16[3,24,768]{2,1,0:T(8,128)(2,1)S(1)}, bf16[3,24,768]{2,1,0:T(8,128)(2,1)S(1)}, u32[]{:S(2)}, u32[]{:S(2)}) collective-permute-start(bf16[3,24,768]{2,1,0:T(8,128)(2,1)S(1)} %get-tuple-element.124), channel_id=1, source_target_pairs={{0,16},{1,17},{2,18},{3,19},{4,20},{5,21},{6,22},{7,23},{8,24},{9,... | collective-permute-start | bytes 331784 | tf_op jit(solution)/shard_map/ppermute | solution.py:115
  106.3 9.3 %collective-permute-start.26 = (bf16[3,24,768]{2,1,0:T(8,128)(2,1)S(1)}, bf16[3,24,768]{2,1,0:T(8,128)(2,1)S(1)}, u32[]{:S(2)}, u32[]{:S(2)}) collective-permute-start(bf16[3,24,768]{2,1,0:T(8,128)(2,1)S(1)} %get-tuple-element.130), channel_id=1, source_target_pairs={{0,16},{1,17},{2,18},{3,19},{4,20},{5,21},{6,22},{7,23},{8,24},{9,... | collective-permute-start | bytes 331784 | tf_op jit(solution)/shard_map/ppermute | solution.py:115
  (8 other events, 56.0 us)
